TPU v7x, 32 devices: a whole 2x2x4 slice. The times are simulated.
32 devices in a mesh: dp: 16 (over z, x, core), seq: 2 (over y).
Axes of the slice: x: 2, y: 2, z: 4, core: 2. Of those that a mesh axis runs over, the one named last changes fastest.
Arguments:
- queries: bfloat16 [16, 768, 1536], P('dp', 'seq'), may hold values from -16 to 16
- key_rows: bfloat16 [16, 768, 1536], P('dp', 'seq'), may hold values from -16 to 16
- value_rows: bfloat16 [16, 768, 1536], P('dp', 'seq'), may hold values from -6 to 6
- out_grad: bfloat16 [16, 768, 1536], P('dp', 'seq'), may hold values from -6 to 6
- w_out: bfloat16 [1536, 1536], P('dp'), may hold values from -0.15625 to 0.15625
- band_start: int32 [16], P('dp'), may hold values from 0 to 1
- window_active: int32 [2, 3], replicated, may hold values from 0 to 1
Outputs:
- query_grad: bfloat16 [16, 768, 1536], P('dp', 'seq')
- key_grad: bfloat16 [16, 768, 1536], P('dp', 'seq')
- value_grad: bfloat16 [16, 768, 1536], P('dp', 'seq')
- weight_grad: float32 [1536, 1536], P('dp')
All inputs are finite; a program needn't handle non-finite values.
Results may differ from a plain program's by a relative error of at most 0.011.
Values may be sent and summed in bfloat16 or wider, within the bound.
A program may use at most 128 MiB of HBM per device.

v0:
```python
import math

import jax
import jax.numpy as jnp
from jax import lax
from jax.sharding import PartitionSpec as P

HEADS = 12
HS = 128


def passed_along(value, axis, steps):
    count = lax.axis_size(axis)
    pairs = [(source, (source + steps) % count) for source in range(count)]
    return lax.ppermute(value, axis, pairs)


def window_mask(window_active, tile_index):
    table_ids = jnp.arange(window_active.shape[0], dtype=jnp.int32)
    picked = (table_ids[None, :] == tile_index[:, None]).astype(jnp.int32)
    flags = jnp.sum(picked[:, :, None] * window_active[None, :, :], axis=1)
    centre = (jnp.arange(3, dtype=jnp.int32) == 1)[None, :]
    return (flags == 1) | centre


def to_pairs(values_in, row_count):
    clip_count = values_in.shape[0]
    shaped = values_in.reshape(clip_count, row_count, HEADS // 2, 2, HS)
    return jnp.transpose(shaped, (0, 2, 3, 1, 4)).reshape(
        clip_count * (HEADS // 2), 2, row_count, HS
    )


def from_pairs(values_in, clip_count, row_count):
    shaped = values_in.reshape(clip_count, HEADS // 2, 2, row_count, HS)
    return jnp.transpose(shaped, (0, 3, 1, 2, 4)).reshape(clip_count, row_count, HEADS * HS)


def attend_pairs(operands):
    query_pair, key_pair, value_pair, key_bias = operands
    score_scale = HS ** (-0.5)
    scores = (
        jnp.einsum("hqd,hkd->hqk", query_pair, key_pair, preferred_element_type=jnp.float32)
        * score_scale
        + key_bias[None, None, :]
    )
    row_max = jnp.max(scores, axis=2, keepdims=True)
    exp_scores = jnp.exp(scores - row_max)
    row_sum = jnp.sum(exp_scores, axis=2, keepdims=True)
    weights = (exp_scores / row_sum).astype(jnp.bfloat16)
    attended = jnp.einsum(
        "hqk,hkd->hqd", weights, value_pair, preferred_element_type=jnp.float32
    ).astype(jnp.bfloat16)
    log_total = row_max[:, :, 0] + jnp.log(row_sum[:, :, 0])
    return (attended, log_total)


def backward_pairs(operands):
    query_pair, key_pair, value_pair, key_bias, attended_pair, grad_pair, log_total = operands
    score_scale = HS ** (-0.5)
    scores = (
        jnp.einsum("hqd,hkd->hqk", query_pair, key_pair, preferred_element_type=jnp.float32)
        * score_scale
        + key_bias[None, None, :]
    )
    prob_full = jnp.exp(scores - log_total[:, :, None])
    row_delta = jnp.sum(grad_pair.astype(jnp.float32) * attended_pair.astype(jnp.float32), axis=2)
    prob_weights = prob_full.astype(jnp.bfloat16)
    value_part = jnp.einsum(
        "hqk,hqd->hkd", prob_weights, grad_pair, preferred_element_type=jnp.float32
    )
    prob_grad = jnp.einsum(
        "hqd,hkd->hqk", grad_pair, value_pair, preferred_element_type=jnp.float32
    )
    score_grad = (prob_full * (prob_grad - row_delta[:, :, None])).astype(jnp.bfloat16)
    query_part = (
        jnp.einsum("hqk,hkd->hqd", score_grad, key_pair, preferred_element_type=jnp.float32)
        * score_scale
    )
    key_part = (
        jnp.einsum("hqk,hqd->hkd", score_grad, query_pair, preferred_element_type=jnp.float32)
        * score_scale
    )
    return (query_part, key_part, value_part)


def per_device(queries, key_rows, value_rows, out_grad, w_out, band_start, window_active):
    clip_count, tile_len, feat_width = queries.shape
    seq_count = lax.axis_size("seq")
    seq_place = lax.axis_index("seq")
    tile_index = jnp.mod(seq_place - band_start, seq_count)
    active = window_mask(window_active, tile_index)
    key_bias = jnp.repeat(jnp.where(active, 0.0, -jnp.inf).astype(jnp.float32), tile_len, axis=1)
    pair_bias = jnp.broadcast_to(
        key_bias[:, None, :], (clip_count, HEADS // 2, 3 * tile_len)
    ).reshape(clip_count * (HEADS // 2), 3 * tile_len)
    own_panel = jnp.stack((key_rows, value_rows))
    received = []
    for step_by in (1, -1):
        received.append(passed_along(own_panel, "seq", step_by))
    band_panel = jnp.concatenate((received[0], own_panel, received[1]), axis=2)
    query_pairs = to_pairs(queries, tile_len)
    key_pairs = to_pairs(band_panel[0], 3 * tile_len)
    value_pairs = to_pairs(band_panel[1], 3 * tile_len)
    attended_pairs, log_totals = lax.map(
        attend_pairs, (query_pairs, key_pairs, value_pairs, pair_bias)
    )
    attended = from_pairs(attended_pairs, clip_count, tile_len).reshape(
        clip_count * tile_len, feat_width
    )
    grad_flat = out_grad.reshape(clip_count * tile_len, out_grad.shape[2])
    attended_grad = lax.dot_general(
        grad_flat,
        lax.all_gather(w_out, "dp", axis=0, tiled=True),
        (((1,), (1,)), ((), ())),
        preferred_element_type=jnp.float32,
    ).astype(jnp.bfloat16)
    all_tokens = clip_count * lax.axis_size("dp") * seq_count * tile_len
    grad_norm = 1.0 / math.sqrt(all_tokens)
    weight_part = lax.psum_scatter(
        lax.dot_general(
            attended, grad_flat, (((0,), (0,)), ((), ())), preferred_element_type=jnp.float32
        )
        * grad_norm,
        "dp",
        scatter_dimension=0,
        tiled=True,
    )
    weight_grad = lax.psum(weight_part, "seq")
    grad_heads = to_pairs(attended_grad.reshape(clip_count, tile_len, feat_width), tile_len)
    query_parts, key_parts, value_parts = lax.map(
        backward_pairs,
        (query_pairs, key_pairs, value_pairs, pair_bias, attended_pairs, grad_heads, log_totals),
    )
    query_grad = from_pairs(query_parts, clip_count, tile_len).astype(jnp.bfloat16)
    key_full = from_pairs(key_parts, clip_count, 3 * tile_len).reshape(
        clip_count, 3, tile_len, feat_width
    )
    value_full = from_pairs(value_parts, clip_count, 3 * tile_len).reshape(
        clip_count, 3, tile_len, feat_width
    )
    both_parts = jnp.stack((key_full, value_full))
    summed = both_parts[:, :, 1]
    for step_by, slot_pos in ((-1, 0), (1, 2)):
        summed = summed + passed_along(both_parts[:, :, slot_pos], "seq", step_by)
    return (query_grad, summed[0].astype(jnp.bfloat16), summed[1].astype(jnp.bfloat16), weight_grad)


def solution(mesh):
    placed = (
        P("dp", "seq", None),
        P("dp", "seq", None),
        P("dp", "seq", None),
        P("dp", "seq", None),
        P("dp", None),
        P("dp"),
        P(),
    )
    return jax.shard_map(
        per_device,
        mesh=mesh,
        in_specs=placed,
        out_specs=(P("dp", "seq", None), P("dp", "seq", None), P("dp", "seq", None), P("dp", None)),
        check_vma=False,
    )
```

profile of v0, /device:TPU:0, one launch (start us, length us, event | category | flops | bytes accessed | tf_op | source)
XLA Modules:
  0.0 510.3 jit_solution(8802815793517698460)
XLA Ops:
  12.5 3.0 collective-permute-start
  16.5 2.4 copy.20
  20.5 46.5 %collective-permute-done = bf16[2,1,384,1536]{2,3,1,0:T(8,128)(2,1)} collective-permute-done((bf16[2,1,384,1536]{2,3,1,0:T(8,128)(2,1)}, bf16[2,1,384,1536]{2,3,1,0:T(8,128)(2,1)}, u32[]{:S(2)}, u32[]{:S(2)}) %collective-permute-start) | collective-permute-done | bytes 2359328 | tf_op jit(solution)/shard_map/ppermute | solution.py:15
  67.0 3.6 pad_maximum_fusion
  70.6 3.3 fusion.52
  74.0 5.8 %copy.25 = bf16[6,2,1152,128]{3,2,1,0:T(8,128)(2,1)} copy(bf16[6,2,1152,128]{2,3,1,0:T(8,128)(2,1)} %bitcast.170) | data formatting | bytes 7077888 | tf_op jit(solution)/shard_map/while | solution.py:105
  79.8 5.9 %copy.28 = bf16[6,2,1152,128]{3,2,1,0:T(8,128)(2,1)} copy(bf16[6,2,1152,128]{2,3,1,0:T(8,128)(2,1)} %bitcast.169) | data formatting | bytes 7077888 | tf_op jit(solution)/shard_map/while | solution.py:131
  86.3 35.7 %while.26 = (s32[]{:T(128)}, bf16[6,2,384,128]{3,2,1,0:T(8,128)(2,1)S(1)}, f32[6,2,384]{2,1,0:T(2,128)}, bf16[6,2,384,128]{3,2,1,0:T(8,128)(2,1)S(1)}, bf16[6,2,...) while((s32[]{:T(128)}, ...), condition=%wide.region_4.5_spmd, body=%wide.region_1.4_spmd.sunk | while | flops 460160256 | bytes 12234329 | solution.py:105
  90.2 2.0 fusion.80
  96.2 2.0 fusion.80
  102.1 2.0 fusion.80
  108.1 2.0 fusion.80
  114.1 2.0 fusion.80
  120.0 2.0 fusion.80
  124.7 5.1 convolution_multiply_fusion.4
  129.9 5.4 %convolution_convert_fusion = bf16[384,1536]{1,0:T(8,128)(2,1)} fusion(bf16[1536,1536]{1,0:T(8,128)(2,1)} %all-gather.2.cloned.1.call-done, bf16[1,384,1536]{2,1,0:T(8,128)(2,1)S(1)} %copy-done), kind=kOutput, calls=%fused_computation.67 | convolution fusion | flops 1812529152 | bytes 7077888 | tf_op jit(solution)/shard_map/dot_general | solution.py:112
  135.3 2.9 reshape_reshape.6
  138.4 74.1 %while.27 = (s32[]{:T(128)}, bf16[6,2,384,128]{3,2,1,0:T(8,128)(2,1)}, f32[6,2,1152,128]{3,2,1,0:T(8,128)}, f32[6,2,1152,128]{3,2,1,0:T(8,128)}, bf16[6,2,384,12...) while((s32[]{:T(128)}, ...), condition=%wide.region_7.8_spmd, body=%wide.region_5.7_spmd.sunk | while | flops 1139440896 | bytes 21664896 | solution.py:131
  139.9 1.9 fusion.91
  148.4 2.5 fusion.94
  152.4 2.0 fusion.91
  157.2 1.9 fusion.95
  159.0 1.9 fusion.96
  161.0 2.4 fusion.94
  164.8 1.9 fusion.91
  169.5 1.9 fusion.95
  173.2 2.4 fusion.94
  177.1 1.9 fusion.91
  183.6 1.9 fusion.96
  185.5 2.4 fusion.94
  189.3 1.9 fusion.91
  194.0 1.9 fusion.95
  195.9 1.9 fusion.96
  197.8 2.4 fusion.94
  201.6 1.9 fusion.91
  208.2 1.9 fusion.96
  210.1 2.4 fusion.94
  212.5 15.4 %copy.31 = f32[1,1152,6,2,128]{4,3,2,1,0:T(2,128)} copy(f32[1,1152,6,2,128]{4,1,3,2,0:T(8,128)} %bitcast.175) | data formatting | bytes 14155776 | tf_op jit(solution)/shard_map/transpose | solution.py:36
  227.9 10.0 %stack_reshape_reshape.6 = f32[1,1,3,384,1536]{4,3,0,2,1:T(8,128)} reshape(f32[1,1152,6,2,128]{4,3,2,1,0:T(2,128)} %copy.31) | data formatting | bytes 14155776 | tf_op jit(solution)/shard_map/stack;reshape;reshape | solution.py:142
  237.9 15.4 %copy.32 = f32[1,1152,6,2,128]{4,3,2,1,0:T(2,128)} copy(f32[1,1152,6,2,128]{4,1,3,2,0:T(8,128)} %bitcast.176) | data formatting | bytes 14155776 | tf_op jit(solution)/shard_map/transpose | solution.py:36
  253.3 10.0 %stack_reshape_reshape.7 = f32[1,1,3,384,1536]{4,3,0,2,1:T(8,128)} reshape(f32[1,1152,6,2,128]{4,3,2,1,0:T(2,128)} %copy.32) | data formatting | bytes 14155776 | tf_op jit(solution)/shard_map/stack;reshape;reshape | solution.py:142
  263.2 3.7 constant_dynamic-update-slice_fusion.1
  268.8 4.4 slice_bitcast_fusion.1
  273.3 3.5 copy-done.2
  281.3 113.1 %collective-permute-done.1 = f32[2,1,384,1536]{3,2,0,1:T(8,128)} collective-permute-done((f32[2,1,384,1536]{3,2,0,1:T(8,128)}, f32[2,1,384,1536]{3,2,0,1:T(8,128)}, u32[]{:S(2)}, u32[]{:S(2)}) %collective-permute-start.1) | collective-permute-done | bytes 4718624 | tf_op jit(solution)/shard_map/ppermute | solution.py:15
  394.4 99.4 %collective-permute-done.2 = f32[2,1,384,1536]{3,2,1,0:T(8,128)} collective-permute-done((f32[2,1,384,1536]{3,2,1,0:T(8,128)}, f32[2,1,384,1536]{3,2,1,0:T(8,128)}, u32[]{:S(2)}, u32[]{:S(2)}) %collective-permute-start.2) | collective-permute-done | bytes 4718624 | tf_op jit(solution)/shard_map/ppermute | solution.py:15
  493.8 6.5 %fusion.48 = bf16[2,1,384,1536]{3,2,1,0:T(8,128)(2,1)S(1)} fusion(f32[2,1,384,1536]{3,2,1,0:T(8,128)} %collective-permute-done.2, f32[2,1,384,1536]{3,2,0,1:T(8,128)} %collective-permute-done.1, f32[2,1,3,384,1536]{4,3,0,2,1:T(8,128)} %copy-done.2), kind=kLoop, calls=%fused_computation.66 | loop fusion | flops 3538944 | bytes 16515072 | tf_op jit(solution)/shard_map/convert.2
  501.9 1.9 copy.70
  (102 shorter events, 77.7 us)
Async XLA Ops:
  7.2 117.6 %copy-start = (bf16[1,384,1536]{2,1,0:T(8,128)(2,1)S(1)}, bf16[1,384,1536]{2,1,0:T(8,128)(2,1)}, u32[]{:S(2)}) copy-start(bf16[1,384,1536]{2,1,0:T(8,128)(2,1)} %param.14) | copy-start | bytes 3538948
  7.2 122.7 %all-gather.2.cloned.1.call-start = ((), (), s32[]{:S(2)}) async-start(), calls=%async_computation.1 | async-start | bytes 5013504 | tf_op jit(solution)/shard_map/all_gather | solution.py:114
  9.0 7.3 %copy-start.8 = (s32[2,3]{1,0:T(2,128)S(1)}, s32[2,3]{1,0:T(2,128)}, u32[]{:S(2)}) copy-start(s32[2,3]{1,0:T(2,128)} %param.17) | copy-start | bytes 76
  10.7 8.1 %copy-start.4 = (bf16[1,384,1536]{1,2,0:T(8,128)(2,1)}, bf16[1,384,1536]{1,2,0:T(8,128)(2,1)S(1)}, u32[]{:S(2)}) copy-start(bf16[1,384,1536]{1,2,0:T(8,128)(2,1)S(1)} %copy.22) | copy-start | bytes 3538948
  12.5 54.5 %collective-permute-start = (bf16[2,1,384,1536]{2,3,1,0:T(8,128)(2,1)}, bf16[2,1,384,1536]{2,3,1,0:T(8,128)(2,1)}, u32[]{:S(2)}, u32[]{:S(2)}) collective-permute-start(bf16[2,1,384,1536]{2,3,1,0:T(8,128)(2,1)} %pad_maximum_fusion.1), channel_id=1, source_target_pairs={{0,1},{1,0},{2,3},{3,2},{4,5},{5,4},{6,7},{7,6},{8,9},{9,8},{10,11... | collective-permute-start | bytes 7077896 | tf_op jit(solution)/shard_map/ppermute | solution.py:15
  15.5 265.8 %reduce-scatter.2.cloned.1.call-start = ((), (), s32[]{:S(2)}) async-start(), calls=%async_computation.2 | async-start | bytes 10027008 | tf_op jit(solution)/shard_map/reduce_scatter | solution.py:120
  79.8 6.5 %copy-start.5 = (bf16[6,2,384,128]{3,2,1,0:T(8,128)(2,1)S(1)}, bf16[6,2,384,128]{3,2,1,0:T(8,128)(2,1)}, u32[]{:S(2)}) copy-start(bf16[6,2,384,128]{3,2,1,0:T(8,128)(2,1)} %custom-call.1) | copy-start | bytes 3538948
  122.0 1.0 copy-start.6
  129.8 372.0 %all-reduce.2.cloned.1.call-start = ((), (), s32[]{:S(2)}) async-start(), calls=%async_computation.3 | async-start | bytes 1179648 | tf_op jit(solution)/shard_map/psum | solution.py:129
  263.2 5.0 copy-start.3
  268.8 7.9 %copy-start.2 = (f32[2,1,3,384,1536]{4,3,0,2,1:T(8,128)}, f32[2,1,3,384,1536]{4,3,0,2,1:T(8,128)S(1)}, u32[]{:S(2)}) copy-start(f32[2,1,3,384,1536]{4,3,0,2,1:T(8,128)S(1)} %constant_dynamic-update-slice_fusion) | copy-start | bytes 42467332
  268.8 10.0 %copy-start.7 = (bf16[6,2,384,128]{3,2,1,0:T(8,128)(2,1)S(1)}, bf16[6,2,384,128]{3,2,1,0:T(8,128)(2,1)}, u32[]{:S(2)}) copy-start(bf16[6,2,384,128]{3,2,1,0:T(8,128)(2,1)} %get-tuple-element.103) | copy-start | bytes 3538948
  276.7 117.7 %collective-permute-start.1 = (f32[2,1,384,1536]{3,2,0,1:T(8,128)}, f32[2,1,384,1536]{3,2,0,1:T(8,128)}, u32[]{:S(2)}, u32[]{:S(2)}) collective-permute-start(f32[2,1,384,1536]{3,2,0,1:T(8,128)} %get-tuple-element.162), channel_id=1, source_target_pairs={{0,1},{1,0},{2,3},{3,2},{4,5},{5,4},{6,7},{7,6},{8,9},{9,8},{10,11... | collective-permute-start | bytes 14155784 | tf_op jit(solution)/shard_map/ppermute | solution.py:15
  278.5 215.3 %collective-permute-start.2 = (f32[2,1,384,1536]{3,2,1,0:T(8,128)}, f32[2,1,384,1536]{3,2,1,0:T(8,128)}, u32[]{:S(2)}, u32[]{:S(2)}) collective-permute-start(f32[2,1,384,1536]{3,2,1,0:T(8,128)} %get-tuple-element.163), channel_id=1, source_target_pairs={{0,1},{1,0},{2,3},{3,2},{4,5},{5,4},{6,7},{7,6},{8,9},{9,8},{10,11... | collective-permute-start | bytes 14155784 | tf_op jit(solution)/shard_map/ppermute | solution.py:15
  493.8 10.0 %copy-start.1 = (bf16[1,384,1536]{2,1,0:T(8,128)(2,1)S(1)}, bf16[1,384,1536]{2,1,0:T(8,128)(2,1)}, u32[]{:S(2)}) copy-start(bf16[1,384,1536]{2,1,0:T(8,128)(2,1)} %param.14) | copy-start | bytes 3538948
Sparse Core Ops, SparseCore 0:
  15.6 53.5 all-gather.1
  130.0 112.7 reduce-scatter.1
  281.4 44.2 all-reduce.1
where the time goes:
time: 514 us; the launch traced here: 510 us
  waiting for transfers between devices  259 us (50%)
  local copies, waits for them, and re-layouts  113 us (22%)
  matrix products  91.4 us (18%)
  other arithmetic  26.9 us (5%)
  between operations  14.6 us (3%)
    ppermute x3, waiting for transfers between devices, passed_along(): return lax.ppermute(value, axis, pairs)  259 us
    transpose x2, local copies, waits for them, and re-layouts, from_pairs(): jnp.transpose(shaped, (0, 3, 1, 2, 4))  30.8 us
    another operation x3, local copies, waits for them, and re-layouts, per_device(): both_parts = jnp.stack((key_full, value_full))  20.5 us
    unnamed x23, local copies, waits for them, and re-layouts  17.3 us
    dot_general x6, matrix products, backward_pairs(): jnp.einsum('hqk,hkd->hqd', score_grad, key_pair, preferred_element_type=j...  14.3 us
    dot_general x6, matrix products, attend_pairs(): jnp.einsum('hqk,hkd->hqd', weights, value_pair, preferred_element_type=jn...  11.8 us
    dot_general x6, matrix products, backward_pairs(): jnp.einsum('hqd,hkd->hqk', query_pair, key_pair, preferred_element_type=j...  11.3 us
    dot_general x6, matrix products, backward_pairs(): jnp.einsum('hqk,hqd->hkd', prob_weights, grad_pair, preferred_element_typ...  11.3 us
  transfers between devices with their start and end apart: 6, of which 3 were waited for; matrix products, arithmetic and copies ran while one was open for 43% of the time, Pallas kernels for 0%

commit v1 on v0

v1 whole, which is shorter than its diff:
```python
import functools
import math

import jax
import jax.numpy as jnp
from jax import lax
from jax.experimental import pallas as pl
from jax.experimental.pallas import tpu as pltpu
from jax.sharding import PartitionSpec as P

HEADS = 12
HS = 128
CHUNKS = (4, 4, 4)
SCALE = HS ** (-0.5)
LOG2E = 1.4426950408889634
VMEM_LIMIT = 48 * 1024 * 1024

NT_DIMS = (((1,), (1,)), ((), ()))
TN_DIMS = (((0,), (0,)), ((), ()))
NN_DIMS = (((1,), (0,)), ((), ()))


def mm(lhs, rhs, dims):
    return lax.dot_general(lhs, rhs, dims, preferred_element_type=jnp.float32)


def passed_along(value, axis, steps):
    count = lax.axis_size(axis)
    pairs = [(source, (source + steps) % count) for source in range(count)]
    return lax.ppermute(value, axis, pairs)


def forward_kernel(other_count, bias_ref, q_ref, k_ref, v_ref, *refs):
    other_refs = refs[:other_count]
    att_ref, lse_ref = refs[-2:]
    query = q_ref[...]
    scores = [mm(k_ref[...], query, NT_DIMS) * (SCALE * LOG2E)]
    values = [v_ref[...]]
    for place, other_ref in enumerate(other_refs):
        scores.append(mm(other_ref[0], query, NT_DIMS) * (SCALE * LOG2E) + bias_ref[place])
        values.append(other_ref[1])
    row_max = functools.reduce(
        jnp.maximum, [jnp.max(block, axis=0, keepdims=True) for block in scores]
    )
    total = 0.0
    mixed = 0.0
    for block, value in zip(scores, values):
        weights = jnp.exp2(block - row_max)
        total = total + jnp.sum(weights, axis=0, keepdims=True)
        mixed = mixed + mm(value, weights.astype(jnp.bfloat16), TN_DIMS)
    att_ref[...] = jnp.transpose(mixed / total).astype(att_ref.dtype)
    lse_ref[0] = jnp.broadcast_to(row_max + jnp.log2(total), lse_ref.shape[1:])


def backward_kernel(
    other_count, bias_ref, q_ref, k_ref, v_ref, att_ref, lse_ref, og_ref, w_ref, *refs
):
    other_refs = refs[:other_count]
    dq_ref, own_ref = refs[-2 - other_count : len(refs) - other_count]
    out_refs = refs[len(refs) - other_count :]
    query = q_ref[...]
    grad = mm(og_ref[...], w_ref[...], NT_DIMS).astype(jnp.bfloat16)
    product = grad.astype(jnp.float32) * att_ref[...].astype(jnp.float32)
    delta = jnp.sum(jnp.transpose(product), axis=0, keepdims=True)
    log_total = lse_ref[0][0:1]
    query_part = 0.0
    for place in range(other_count + 1):
        if place == 0:
            key, value, shift = k_ref[...], v_ref[...], log_total
        else:
            key, value = other_refs[place - 1][0], other_refs[place - 1][1]
            shift = log_total - bias_ref[place - 1]
        prob = jnp.exp2(mm(key, query, NT_DIMS) * (SCALE * LOG2E) - shift)
        value_part = mm(prob.astype(jnp.bfloat16), grad, NN_DIMS)
        score_grad = (prob * (mm(value, grad, NT_DIMS) - delta)).astype(jnp.bfloat16)
        key_part = mm(score_grad, query, NN_DIMS) * SCALE
        query_part = query_part + mm(key, score_grad, TN_DIMS)
        target = own_ref if place == 0 else out_refs[place - 1]
        target[0] = key_part.astype(target.dtype)
        target[1] = value_part.astype(target.dtype)
    dq_ref[...] = jnp.transpose(query_part * SCALE).astype(dq_ref.dtype)


def add_kernel(other_count, own_ref, *refs):
    dk_ref, dv_ref = refs[-2:]
    keys, values = own_ref[0], own_ref[1]
    for ref in refs[:other_count]:
        keys = keys + ref[0].astype(jnp.float32)
        values = values + ref[1].astype(jnp.float32)
    dk_ref[...] = keys.astype(dk_ref.dtype)
    dv_ref[...] = values.astype(dv_ref.dtype)


def params():
    return pltpu.CompilerParams(vmem_limit_bytes=VMEM_LIMIT)


def cost(flops, moved, exps):
    return pl.CostEstimate(flops=int(flops), bytes_accessed=int(moved), transcendentals=int(exps))


def column_block(rows, first):
    return pl.BlockSpec((rows, HS), lambda i: (0, first + i))


def pair_block(rows):
    return pl.BlockSpec((2, rows, HS), lambda i: (0, 0, i))


SMEM_BLOCK = pl.BlockSpec(memory_space=pltpu.SMEM)
HBM_BLOCK = pl.BlockSpec(memory_space=pl.ANY)


def forward(first, heads, bias, q, k, v, others, att):
    rows, width = q.shape
    count = len(others)
    head = column_block(rows, first)
    chained = [] if att is None else [att]
    return pl.pallas_call(
        functools.partial(forward_kernel, count),
        grid=(heads,),
        in_specs=[SMEM_BLOCK, head, head, head]
        + [pair_block(rows)] * count
        + [HBM_BLOCK] * len(chained),
        out_specs=[head, pl.BlockSpec((1, 8, rows), lambda i: (i, 0, 0))],
        out_shape=[
            jax.ShapeDtypeStruct((rows, width), jnp.bfloat16),
            jax.ShapeDtypeStruct((heads, 8, rows), jnp.float32),
        ],
        input_output_aliases={4 + count: 0} if chained else {},
        compiler_params=params(),
        cost_estimate=cost(
            heads * (count + 1) * rows * rows * HS * 4,
            heads * rows * HS * 2 * (4 + 2 * count),
            heads * (count + 1) * rows * rows,
        ),
        name="attend",
    )(bias, q, k, v, *others, *chained)


def backward(first, heads, bias, q, k, v, att, lse, og, w, others, dq):
    rows, width = q.shape
    count = len(others)
    head = column_block(rows, first)
    chained = [] if dq is None else [dq]
    results = pl.pallas_call(
        functools.partial(backward_kernel, count),
        grid=(heads,),
        in_specs=[SMEM_BLOCK, head, head, head, head]
        + [
            pl.BlockSpec((1, 8, rows), lambda i: (i, 0, 0)),
            pl.BlockSpec(og.shape, lambda i: (0, 0)),
            pl.BlockSpec((HS, w.shape[1]), lambda i: (first + i, 0)),
        ]
        + [pair_block(rows)] * count
        + [HBM_BLOCK] * len(chained),
        out_specs=[head] + [pair_block(rows)] * (count + 1),
        out_shape=[
            jax.ShapeDtypeStruct((rows, width), jnp.bfloat16),
            jax.ShapeDtypeStruct((2, rows, heads * HS), jnp.float32),
        ]
        + [jax.ShapeDtypeStruct((2, rows, heads * HS), jnp.bfloat16)] * count,
        input_output_aliases={8 + count: 0} if chained else {},
        compiler_params=params(),
        cost_estimate=cost(
            heads * ((count + 1) * rows * rows * HS * 10 + rows * HS * width * 2),
            heads * rows * HS * 2 * (8 + 8 * count),
            heads * (count + 1) * rows * rows,
        ),
        name="attend_grad",
    )(bias, q, k, v, att, lse, og, w, *others, *chained)
    return results[0], results[1], results[2:]


def add_parts(first, heads, rows, width, own, received, chained):
    count = len(received)
    head = column_block(rows, first)
    return pl.pallas_call(
        functools.partial(add_kernel, count),
        grid=(heads,),
        in_specs=[pair_block(rows)] * (count + 1) + [HBM_BLOCK] * len(chained),
        out_specs=[head, head],
        out_shape=[jax.ShapeDtypeStruct((rows, width), jnp.bfloat16)] * 2,
        input_output_aliases={1 + count: 0, 2 + count: 1} if chained else {},
        compiler_params=params(),
        cost_estimate=cost(0, heads * rows * HS * 2 * (6 + 2 * count), 0),
        name="add_parts",
    )(own, *received, *chained)


def exchange_bit(value, bit):
    count = lax.axis_size("dp")
    return lax.ppermute(value, "dp", [(source, source ^ (1 << bit)) for source in range(count)])


def summed_rows(att, og, norm):
    place = lax.axis_index("dp")
    bits = lax.axis_size("dp").bit_length() - 1
    rows, width = att.shape
    block = width >> bits
    core = lax.rem(place, 2)
    panels = att.reshape(rows, width // (2 * block), 2, block)

    def side(which):
        return lax.dynamic_index_in_dim(panels, which, 2, keepdims=False).reshape(rows, width // 2)

    mine, theirs = side(core), side(1 - core)
    half = og.shape[1] // 2
    orders = (tuple(range(1, bits)), tuple(range(2, bits)) + (1,))
    halves = []
    for part, order in enumerate(orders):
        columns = og[:, part * half : (part + 1) * half]
        sent = exchange_bit((mm(theirs, columns, TN_DIMS) * norm).astype(jnp.bfloat16), 0)
        held = mm(mine, columns, TN_DIMS) * norm + sent.astype(jnp.float32)
        left = list(range(bits - 1, 0, -1))
        held = held.reshape((2,) * len(left) + (block, half))
        for bit in order:
            spot = left.index(bit)
            own = lax.rem(lax.div(place, 1 << bit), 2)
            away = lax.dynamic_index_in_dim(held, 1 - own, spot, keepdims=False)
            kept = lax.dynamic_index_in_dim(held, own, spot, keepdims=False)
            held = kept + exchange_bit(away.astype(jnp.bfloat16), bit).astype(jnp.float32)
            left.remove(bit)
        halves.append(held)
    return halves


def per_device(queries, key_rows, value_rows, out_grad, w_out, band_start, window_active):
    clip_count, tile_len, width = queries.shape
    seq_count = lax.axis_size("seq")
    seq_place = lax.axis_index("seq")
    steps = (1,) if seq_count == 2 else (1, -1)
    tile_index = jnp.mod(seq_place - band_start, seq_count)
    flags = (window_active[tile_index] == 1).astype(jnp.int32)
    times = (flags[:, 0] + flags[:, 2])[:, None] if seq_count == 2 else flags[:, 0::2]
    biases = jnp.where(times == 0, -jnp.inf, jnp.where(times == 2, 1.0, 0.0)).astype(jnp.float32)
    w_full = lax.all_gather(w_out, "dp", axis=0, tiled=True)
    spans = []
    first = 0
    for heads in CHUNKS:
        spans.append((first, heads))
        first += heads

    def cut(array, span):
        return array[:, span[0] * HS : (span[0] + span[1]) * HS]

    outs = []
    weight = None
    norm = 1.0 / math.sqrt(clip_count * lax.axis_size("dp") * seq_count * tile_len)
    for clip in range(clip_count):
        q, k, v, og = queries[clip], key_rows[clip], value_rows[clip], out_grad[clip]
        bias = biases[clip]
        others = []
        for span in spans:
            panel = jnp.stack((cut(k, span), cut(v, span)))
            others.append([passed_along(panel, "seq", step) for step in steps])
        att, lses = None, []
        for span, other in zip(spans, others):
            att, lse = forward(*span, bias, q, k, v, other, att)
            lses.append(lse)
        part = summed_rows(att, og, norm)
        weight = part if weight is None else [a + b for a, b in zip(weight, part)]
        dq, sums = None, ()
        pending = []
        for span, other, lse in zip(spans, others, lses):
            dq, own, away = backward(*span, bias, q, k, v, att, lse, og, w_full, other, dq)
            received = [passed_along(x, "seq", -step) for x, step in zip(away, steps)]
            pending.append((span, own, received))
        for span, own, received in pending:
            sums = add_parts(*span, tile_len, width, own, received, sums)
        outs.append((dq, *sums))
    if seq_count == 2:
        weight = [half.astype(jnp.bfloat16) for half in weight]
        weight = [
            half.astype(jnp.float32) + passed_along(half, "seq", 1).astype(jnp.float32)
            for half in weight
        ]
    else:
        weight = [lax.psum(half, "seq") for half in weight]
    grads = [jnp.stack(group) if clip_count > 1 else group[0][None] for group in zip(*outs)]
    return (*grads, jnp.concatenate(weight, axis=1))


def solution(mesh):
    rows = P("dp", "seq", None)
    return jax.shard_map(
        per_device,
        mesh=mesh,
        in_specs=(rows, rows, rows, rows, P("dp", None), P("dp"), P()),
        out_specs=(rows, rows, rows, P("dp", None)),
        check_vma=False,
    )
```

time: 514 us -> 210 us (0.41)
  waiting for transfers between devices: 259 us -> 89.8 us
  local copies, waits for them, and re-layouts: 113 us -> 15.6 us
  matrix products: 91.4 us -> 8.06 us
  Pallas kernels: 0 us -> 49.7 us
  other arithmetic: 26.9 us -> 9.24 us
  starting transfers between devices: 5.11 us -> 20.9 us
    ppermute x3 -> x8, waiting for transfers between devices: 259 us -> 60.7 us  [passed_along(): return lax.ppermute(value, axis, pairs)]
    dot_general x44 -> x4, matrix products: 91.4 us -> 8.06 us  [mm(): return lax.dot_general(lhs, rhs, dims, preferred_element_type=jnp.float32)]
    pallas_call x0 -> x9, Pallas kernels: none -> 49.7 us  [the longest x3 30.7 us: backward(): pl.pallas_call(functools.partial(backward_kernel, count), grid=(heads,),...]
    transpose x2 -> x0, local copies, waits for them, and re-layouts: 30.8 us -> none  [from_pairs(): jnp.transpose(shaped, (0, 3, 1, 2, 4))]
    ppermute x0 -> x8, waiting for transfers between devices: none -> 28.4 us  [exchange_bit(): lax.ppermute(value, 'dp', [(source, source ^ 1 << bit) for source in rang...]
    another operation x5 -> x1, local copies, waits for them, and re-layouts: 23.6 us -> 1.89 us  [per_device(): panel = jnp.stack((cut(k, span), cut(v, span)))]
    while x4 -> x0, local copies, waits for them, and re-layouts: 15.1 us -> none  [the longest x2 7.58 us: per_device(): lax.map(backward_pairs, (query_pairs, key_pairs, value_pairs, pair_bias,...]
    reduce_sum x13 -> x0, other arithmetic: 11.4 us -> none  [the longest x6 6.74 us: backward_pairs(): jnp.sum(grad_pair.astype(jnp.float32) * attended_pair.astype(jnp.float32)...]
  transfers between devices with their start and end apart: 6 -> 17, of which waited for: 3 -> 9; matrix products, arithmetic and copies ran while one was open for 43% -> 13% of each run, Pallas kernels for 0% -> 23%
where the time goes in v1:
time: 210 us; the launch traced here: 209 us
  waiting for transfers between devices  89.8 us (43%)
  Pallas kernels  49.7 us (24%)
  starting transfers between devices  20.9 us (10%)
  between operations  16.2 us (8%)
  local copies, waits for them, and re-layouts  15.6 us (7%)
  other arithmetic  9.24 us (4%)
  matrix products  8.06 us (4%)
    ppermute x8, waiting for transfers between devices, passed_along(): return lax.ppermute(value, axis, pairs)  60.7 us
    pallas_call x3, Pallas kernels, backward(): pl.pallas_call(functools.partial(backward_kernel, count), grid=(heads,),...  30.7 us
    ppermute x8, waiting for transfers between devices, exchange_bit(): lax.ppermute(value, 'dp', [(source, source ^ 1 << bit) for source in rang...  28.4 us
    pallas_call x3, Pallas kernels, forward(): pl.pallas_call(functools.partial(forward_kernel, count), grid=(heads,), i...  13.7 us
    ppermute x8, starting transfers between devices, passed_along(): return lax.ppermute(value, axis, pairs)  10.6 us
    ppermute x8, starting transfers between devices, exchange_bit(): lax.ppermute(value, 'dp', [(source, source ^ 1 << bit) for source in rang...  10.2 us
    dot_general x4, matrix products, mm(): return lax.dot_general(lhs, rhs, dims, preferred_element_type=jnp.float32)  8.06 us
    unnamed x44, local copies, waits for them, and re-layouts  5.98 us
  transfers between devices with their start and end apart: 17, of which 9 were waited for; matrix products, arithmetic and copies ran while one was open for 13% of the time, Pallas kernels for 23%

profile of v1, /device:TPU:0, one launch (start us, length us, event | category | flops | bytes accessed | tf_op | source)
XLA Modules:
  0.0 209.5 jit_solution(10294606803949194742)
XLA Ops:
  7.9 1.9 slice_bitcast_fusion
  9.8 0.9 pad_maximum_fusion.2
  10.8 3.0 %collective-permute-start.2 = (bf16[2,384,512]{2,1,0:T(8,128)(2,1)}, bf16[2,384,512]{2,1,0:T(8,128)(2,1)}, u32[]{:S(2)}, u32[]{:S(2)}) collective-permute-start(bf16[2,384,512]{2,1,0:T(8,128)(2,1)} %pad_maximum_fusion.2), channel_id=1, source_target_pairs={{0,1},{1,0},{2,3},{3,2},{4,5},{5,4},{6,7},{7,6},{8,9},{9,8},{10,11... | collective-permute-start | bytes 2359304 | tf_op jit(solution)/shard_map/ppermute | solution.py:30
  13.7 0.9 pad_maximum_fusion.1
  14.7 0.9 pad_maximum_fusion
  15.6 2.0 collective-permute-start
  20.2 12.2 %collective-permute-done.2.refs_0_ = bf16[2,384,512]{2,1,0:T(8,128)(2,1)} collective-permute-done((bf16[2,384,512]{2,1,0:T(8,128)(2,1)}, bf16[2,384,512]{2,1,0:T(8,128)(2,1)}, u32[]{:S(2)}, u32[]{:S(2)}) %collective-permute-start.2) | collective-permute-done | bytes 786464 | tf_op jit(solution)/shard_map/ppermute | solution.py:30
  32.4 4.5 %attend.3 = (bf16[384,1536]{1,0:T(8,128)(2,1)S(1)}, f32[4,8,384]{2,1,0:T(8,128)S(1)}) custom-call(f32[1]{0:T(128)} %bitcast.2.bias_ref, bf16[384,1536]{1,0:T(8,128)(2,1)S(1)} %bitcast.77, bf16[384,1536]{1,0:T(8,128)(2,1)S(1)} %bitcast.64, bf16[384,1536]{1,0:T(8,128)(2,1)S(1)} %bitcast.71, bf16[2,384,512]{2,1,0:T(8,128)(2,1)} %collective-permute-done.2.refs_0_), custom_call_target="tpu_custom_call" | custom-call | flops 603979776 | bytes 2359296 | tf_op jit(solution)/shard_map/attend/pallas_call | solution.py:119
  37.6 11.7 %collective-permute-done.1.refs_0_ = bf16[2,384,512]{2,1,0:T(8,128)(2,1)} collective-permute-done((bf16[2,384,512]{2,1,0:T(8,128)(2,1)}, bf16[2,384,512]{2,1,0:T(8,128)(2,1)}, u32[]{:S(2)}, u32[]{:S(2)}) %collective-permute-start.1) | collective-permute-done | bytes 786464 | tf_op jit(solution)/shard_map/ppermute | solution.py:30
  49.3 4.6 %attend.4 = (bf16[384,1536]{1,0:T(8,128)(2,1)S(1)}, f32[4,8,384]{2,1,0:T(8,128)S(1)}) custom-call(f32[1]{0:T(128)} %bitcast.2.bias_ref, bf16[384,1536]{1,0:T(8,128)(2,1)S(1)} %bitcast.78, bf16[384,1536]{1,0:T(8,128)(2,1)S(1)} %bitcast.65, bf16[384,1536]{1,0:T(8,128)(2,1)S(1)} %bitcast.72, ...), custom_call_target="tpu_custom_call", output_to_operand_aliasing={{0}: (5, {})} | custom-call | flops 603979776 | bytes 2359296 | tf_op jit(solution)/shard_map/attend/pallas_call | solution.py:119
  54.5 10.8 %collective-permute-done.refs_0_ = bf16[2,384,512]{2,1,0:T(8,128)(2,1)} collective-permute-done((bf16[2,384,512]{2,1,0:T(8,128)(2,1)}, bf16[2,384,512]{2,1,0:T(8,128)(2,1)}, u32[]{:S(2)}, u32[]{:S(2)}) %collective-permute-start) | collective-permute-done | bytes 786464 | tf_op jit(solution)/shard_map/ppermute | solution.py:30
  65.3 4.5 %attend.5 = (bf16[384,1536]{1,0:T(8,128)(2,1)S(1)}, f32[4,8,384]{2,1,0:T(8,128)S(1)}) custom-call(f32[1]{0:T(128)} %bitcast.2.bias_ref, bf16[384,1536]{1,0:T(8,128)(2,1)S(1)} %bitcast.79, bf16[384,1536]{1,0:T(8,128)(2,1)S(1)} %bitcast.66, bf16[384,1536]{1,0:T(8,128)(2,1)S(1)} %bitcast.73, ...), custom_call_target="tpu_custom_call", output_to_operand_aliasing={{0}: (5, {})} | custom-call | flops 603979776 | bytes 2359296 | tf_op jit(solution)/shard_map/attend/pallas_call | solution.py:119
  69.8 1.0 copy-done.3
  71.5 2.4 %copy.22 = bf16[384,1536]{0,1:T(8,128)(2,1)} copy(bf16[384,1536]{1,0:T(8,128)(2,1)} %copy-done.3) | data formatting | bytes 2359296 | tf_op jit(solution)/shard_map/attend/pallas_call | solution.py:119
  73.8 2.3 %constant_dynamic-slice_fusion.4 = (bf16[384,8,1,96]{0,3,2,1:T(8,128)(2,1)}, bf16[384,8,1,96]{0,3,2,1:T(8,128)(2,1)S(1)}) fusion(bf16[384,8,2,96]{0,3,2,1:T(8,128)(2,1)} %bitcast.97, s32[]{:T(128)S(6)} %select_n.60, s32[]{:T(128)S(6)} %select_n.61), kind=kLoop, calls=%fused_computation.44 | loop fusion | bytes 2359304 | tf_op jit(solution)/shard_map/jit(dynamic_index_in_dim)/dynamic_slice | solution.py:205
  76.1 1.8 multiply_convert_fusion.1
  77.9 1.8 multiply_convert_fusion
  80.2 0.9 collective-permute-done.6
  81.1 2.5 %convert_add_fusion.1 = f32[768,768]{1,0:T(8,128)S(1)} fusion(bf16[768,768]{1,0:T(8,128)(2,1)} %collective-permute-done.6, bf16[384,768]{0,1:T(8,128)(2,1)} %bitcast.94, bf16[384,1536]{1,0:T(8,128)(2,1)} %bitcast.83), kind=kOutput, calls=%fused_computation.2 | convolution fusion | flops 454754304 | bytes 4718592 | tf_op jit(solution)/shard_map/dot_general | solution.py:24
  83.6 0.9 fusion
  84.5 1.7 collective-permute-start.7
  86.2 2.0 convert_add_fusion
  88.3 1.5 copy-done.15
  89.7 0.9 fusion.1
  90.6 1.6 collective-permute-start.12
  92.2 8.0 %collective-permute-done.7 = bf16[2,2,96,768]{3,2,0,1:T(8,128)(2,1)} collective-permute-done((bf16[2,2,96,768]{3,2,0,1:T(8,128)(2,1)}, bf16[2,2,96,768]{3,2,0,1:T(8,128)(2,1)}, u32[]{:S(2)}, u32[]{:S(2)}) %collective-permute-start.7) | collective-permute-done | bytes 589856 | tf_op jit(solution)/shard_map/ppermute | solution.py:193
  100.1 1.6 bitcast_add_fusion.1
  101.8 1.9 collective-permute-start.8
  103.6 3.5 %collective-permute-done.12 = bf16[2,2,96,768]{3,2,1,0:T(8,128)(2,1)} collective-permute-done((bf16[2,2,96,768]{3,2,1,0:T(8,128)(2,1)}, bf16[2,2,96,768]{3,2,1,0:T(8,128)(2,1)}, u32[]{:S(2)}, u32[]{:S(2)}) %collective-permute-start.12) | collective-permute-done | bytes 589856 | tf_op jit(solution)/shard_map/ppermute | solution.py:193
  107.1 1.2 bitcast_add_fusion
  108.4 2.6 %collective-permute-start.13 = (bf16[2,96,768]{2,1,0:T(8,128)(2,1)S(1)}, bf16[2,96,768]{2,1,0:T(8,128)(2,1)S(1)}, u32[]{:S(2)}, u32[]{:S(2)}) collective-permute-start(bf16[2,96,768]{2,1,0:T(8,128)(2,1)S(1)} %fusion.7), channel_id=1, source_target_pairs={{0,16},{2,18},{4,20},{6,22},{8,24},{10,26},{12,28},{14,30},{16,0},... | collective-permute-start | bytes 884744 | tf_op jit(solution)/shard_map/ppermute | solution.py:193
  111.0 5.7 %collective-permute-done.8 = bf16[2,96,768]{2,1,0:T(8,128)(2,1)S(1)} collective-permute-done((bf16[2,96,768]{2,1,0:T(8,128)(2,1)S(1)}, bf16[2,96,768]{2,1,0:T(8,128)(2,1)S(1)}, u32[]{:S(2)}, u32[]{:S(2)}) %collective-permute-start.8) | collective-permute-done | bytes 294944 | tf_op jit(solution)/shard_map/ppermute | solution.py:193
  116.9 10.3 %collective-permute-done.13 = bf16[2,96,768]{2,1,0:T(8,128)(2,1)S(1)} collective-permute-done((bf16[2,96,768]{2,1,0:T(8,128)(2,1)S(1)}, bf16[2,96,768]{2,1,0:T(8,128)(2,1)S(1)}, u32[]{:S(2)}, u32[]{:S(2)}) %collective-permute-start.13) | collective-permute-done | bytes 294944 | tf_op jit(solution)/shard_map/ppermute | solution.py:193
  127.3 0.8 copy-done.19
  128.8 1.8 collective-permute-start.14
  131.3 1.5 collective-permute-start.10
  133.6 10.2 %attend_grad.3 = (bf16[384,1536]{1,0:T(8,128)(2,1)}, f32[2,384,512]{2,1,0:T(8,128)}, bf16[2,384,512]{2,1,0:T(8,128)(2,1)S(1)}) custom-call(f32[1]{0:T(128)} %bitcast.2.bias_ref, bf16[384,1536]{1,0:T(8,128)(2,1)S(1)} %bitcast.80, bf16[384,1536]{1,0:T(8,128)(2,1)S(1)} %bitcast.67, bf16[384,1536]{1,0:T(8,128)(2,1)S(1)} %bitcast.74, ...), custom_call_target="tpu_custom_call" | custom-call | flops 2113929216 | bytes 6291456 | tf_op jit(solution)/shard_map/attend_grad/pallas_call | solution.py:146
  144.3 10.2 %attend_grad.4 = (bf16[384,1536]{1,0:T(8,128)(2,1)}, f32[2,384,512]{2,1,0:T(8,128)}, bf16[2,384,512]{2,1,0:T(8,128)(2,1)S(1)}) custom-call(f32[1]{0:T(128)} %bitcast.2.bias_ref, bf16[384,1536]{1,0:T(8,128)(2,1)S(1)} %bitcast.81, bf16[384,1536]{1,0:T(8,128)(2,1)S(1)} %bitcast.68, bf16[384,1536]{1,0:T(8,128)(2,1)S(1)} %bitcast.75, ...), custom_call_target="tpu_custom_call", output_to_operand_aliasing={{0}: (9, {})} | custom-call | flops 2113929216 | bytes 6291456 | tf_op jit(solution)/shard_map/attend_grad/pallas_call | solution.py:146
  154.6 1.5 collective-permute-start.4
  156.1 10.3 %attend_grad.5 = (bf16[384,1536]{1,0:T(8,128)(2,1)}, f32[2,384,512]{2,1,0:T(8,128)}, bf16[2,384,512]{2,1,0:T(8,128)(2,1)S(1)}) custom-call(f32[1]{0:T(128)} %bitcast.2.bias_ref, bf16[384,1536]{1,0:T(8,128)(2,1)S(1)} %bitcast.82, bf16[384,1536]{1,0:T(8,128)(2,1)S(1)} %bitcast.69, bf16[384,1536]{1,0:T(8,128)(2,1)S(1)} %bitcast.76, ...), custom_call_target="tpu_custom_call", output_to_operand_aliasing={{0}: (9, {})} | custom-call | flops 2113929216 | bytes 6291456 | tf_op jit(solution)/shard_map/attend_grad/pallas_call | solution.py:146
  166.9 0.9 fusion.8
  167.8 1.6 collective-permute-start.15
  169.4 1.0 convert_add_fusion.3
  170.4 26.0 %collective-permute-done.15 = bf16[96,768]{1,0:T(8,128)(2,1)S(1)} collective-permute-done((bf16[96,768]{1,0:T(8,128)(2,1)S(1)}, bf16[96,768]{1,0:T(8,128)(2,1)S(1)}, u32[]{:S(2)}, u32[]{:S(2)}) %collective-permute-start.15) | collective-permute-done | bytes 147488 | tf_op jit(solution)/shard_map/ppermute | solution.py:30
  196.5 0.9 pad_maximum_fusion.3
  197.4 1.7 add_parts.3
  199.1 1.8 add_parts.4
  200.9 1.8 add_parts.5
  (67 shorter events, 7.2 us)
Async XLA Ops:
  7.2 125.6 %all-gather.2.cloned.1.call-start = ((), (), s32[]{:S(2)}) async-start(), calls=%async_computation | async-start | bytes 5013504 | tf_op jit(solution)/shard_map/all_gather | solution.py:237
  9.8 22.6 %copy-start.2 = (bf16[1,384,1536]{2,1,0:T(8,128)(2,1)S(1)}, bf16[1,384,1536]{2,1,0:T(8,128)(2,1)}, u32[]{:S(2)}) copy-start(bf16[1,384,1536]{2,1,0:T(8,128)(2,1)} %param.7) | copy-start | bytes 3538948
  10.8 21.6 %collective-permute-start.2 = (bf16[2,384,512]{2,1,0:T(8,128)(2,1)}, bf16[2,384,512]{2,1,0:T(8,128)(2,1)}, u32[]{:S(2)}, u32[]{:S(2)}) collective-permute-start(bf16[2,384,512]{2,1,0:T(8,128)(2,1)} %pad_maximum_fusion.2), channel_id=1, source_target_pairs={{0,1},{1,0},{2,3},{3,2},{4,5},{5,4},{6,7},{7,6},{8,9},{9,8},{10,11... | collective-permute-start | bytes 2359304 | tf_op jit(solution)/shard_map/ppermute | solution.py:30
  13.7 18.7 %copy-start.1 = (bf16[1,384,1536]{2,1,0:T(8,128)(2,1)S(1)}, bf16[1,384,1536]{2,1,0:T(8,128)(2,1)}, u32[]{:S(2)}) copy-start(bf16[1,384,1536]{2,1,0:T(8,128)(2,1)} %param.9) | copy-start | bytes 3538948
  14.7 3.7 %copy-start.21 = (s32[2,3]{1,0:T(2,128)S(1)}, s32[2,3]{1,0:T(2,128)}, u32[]{:S(2)}) copy-start(s32[2,3]{1,0:T(2,128)} %param.13) | copy-start | bytes 76
  14.7 17.7 %copy-start = (bf16[1,384,1536]{2,1,0:T(8,128)(2,1)S(1)}, bf16[1,384,1536]{2,1,0:T(8,128)(2,1)}, u32[]{:S(2)}) copy-start(bf16[1,384,1536]{2,1,0:T(8,128)(2,1)} %param.8) | copy-start | bytes 3538948
  14.7 34.6 %collective-permute-start.1 = (bf16[2,384,512]{2,1,0:T(8,128)(2,1)}, bf16[2,384,512]{2,1,0:T(8,128)(2,1)}, u32[]{:S(2)}, u32[]{:S(2)}) collective-permute-start(bf16[2,384,512]{2,1,0:T(8,128)(2,1)} %pad_maximum_fusion.1), channel_id=1, source_target_pairs={{0,1},{1,0},{2,3},{3,2},{4,5},{5,4},{6,7},{7,6},{8,9},{9,8},{10,11... | collective-permute-start | bytes 2359304 | tf_op jit(solution)/shard_map/ppermute | solution.py:30
  15.6 49.7 %collective-permute-start = (bf16[2,384,512]{2,1,0:T(8,128)(2,1)}, bf16[2,384,512]{2,1,0:T(8,128)(2,1)}, u32[]{:S(2)}, u32[]{:S(2)}) collective-permute-start(bf16[2,384,512]{2,1,0:T(8,128)(2,1)} %pad_maximum_fusion), channel_id=1, source_target_pairs={{0,1},{1,0},{2,3},{3,2},{4,5},{5,4},{6,7},{7,6},{8,9},{9,8},{10,11... | collective-permute-start | bytes 2359304 | tf_op jit(solution)/shard_map/ppermute | solution.py:30
  37.0 0.6 copy-start.11
  53.8 0.6 copy-start.9
  69.8 1.0 copy-start.3
  70.9 0.6 copy-start.7
  73.8 2.3 %copy-start.13 = (bf16[1,384,1536]{2,1,0:T(8,128)(2,1)S(1)}, bf16[1,384,1536]{2,1,0:T(8,128)(2,1)}, u32[]{:S(2)}) copy-start(bf16[1,384,1536]{2,1,0:T(8,128)(2,1)} %param.10) | copy-start | bytes 3538948
  77.9 3.2 %collective-permute-start.6 = (bf16[768,768]{1,0:T(8,128)(2,1)}, bf16[768,768]{1,0:T(8,128)(2,1)}, u32[]{:S(2)}, u32[]{:S(2)}) collective-permute-start(bf16[768,768]{1,0:T(8,128)(2,1)} %multiply_convert_fusion.1), channel_id=1, source_target_pairs={{0,2},{2,0},{4,6},{6,4},{8,10},{10,8},{12,14},{14,12},{16,18},{18,... | collective-permute-start | bytes 3538952 | tf_op jit(solution)/shard_map/ppermute | solution.py:193
  79.7 6.5 %collective-permute-start.11 = (bf16[768,768]{1,0:T(8,128)(2,1)}, bf16[768,768]{1,0:T(8,128)(2,1)}, u32[]{:S(2)}, u32[]{:S(2)}) collective-permute-start(bf16[768,768]{1,0:T(8,128)(2,1)} %multiply_convert_fusion), channel_id=1, source_target_pairs={{0,2},{2,0},{4,6},{6,4},{8,10},{10,8},{12,14},{14,12},{16,18},{18,... | collective-permute-start | bytes 3538952 | tf_op jit(solution)/shard_map/ppermute | solution.py:193
  81.1 5.1 %copy-start.18 = (bf16[384,8,1,96]{0,3,2,1:T(8,128)(2,1)S(1)}, bf16[384,8,1,96]{0,3,2,1:T(8,128)(2,1)}, u32[]{:S(2)}) copy-start(bf16[384,8,1,96]{0,3,2,1:T(8,128)(2,1)} %get-tuple-element.57) | copy-start | bytes 1769476
  83.6 2.6 %copy-start.17 = (f32[768,768]{1,0:T(8,128)}, f32[768,768]{1,0:T(8,128)S(1)}, u32[]{:S(2)}) copy-start(f32[768,768]{1,0:T(8,128)S(1)} %convert_add_fusion.1) | copy-start | bytes 7077892
  83.6 2.6 %copy-start.14 = (bf16[1,384,1536]{2,1,0:T(8,128)(2,1)S(1)}, bf16[1,384,1536]{2,1,0:T(8,128)(2,1)}, u32[]{:S(2)}) copy-start(bf16[1,384,1536]{2,1,0:T(8,128)(2,1)} %param.10) | copy-start | bytes 3538948
  84.5 15.7 %collective-permute-start.7 = (bf16[2,2,96,768]{3,2,0,1:T(8,128)(2,1)}, bf16[2,2,96,768]{3,2,0,1:T(8,128)(2,1)}, u32[]{:S(2)}, u32[]{:S(2)}) collective-permute-start(bf16[2,2,96,768]{3,2,0,1:T(8,128)(2,1)} %fusion), channel_id=1, source_target_pairs={{0,4},{2,6},{4,0},{6,2},{8,12},{10,14},{12,8},{14,10},{16,20},{18,... | collective-permute-start | bytes 1769480 | tf_op jit(solution)/shard_map/ppermute | solution.py:193
  88.2 1.5 copy-start.15
  90.6 16.5 %collective-permute-start.12 = (bf16[2,2,96,768]{3,2,1,0:T(8,128)(2,1)}, bf16[2,2,96,768]{3,2,1,0:T(8,128)(2,1)}, u32[]{:S(2)}, u32[]{:S(2)}) collective-permute-start(bf16[2,2,96,768]{3,2,1,0:T(8,128)(2,1)} %fusion.1), channel_id=1, source_target_pairs={{0,8},{2,10},{4,12},{6,14},{8,0},{10,2},{12,4},{14,6},{16,24},{18,... | collective-permute-start | bytes 1769480 | tf_op jit(solution)/shard_map/ppermute | solution.py:193
  92.2 15.0 %copy-start.16 = (f32[768,768]{1,0:T(8,128)S(1)}, f32[768,768]{1,0:T(8,128)}, u32[]{:S(2)}) copy-start(f32[768,768]{1,0:T(8,128)} %copy-done.15) | copy-start | bytes 7077892
  101.8 15.0 %collective-permute-start.8 = (bf16[2,96,768]{2,1,0:T(8,128)(2,1)S(1)}, bf16[2,96,768]{2,1,0:T(8,128)(2,1)S(1)}, u32[]{:S(2)}, u32[]{:S(2)}) collective-permute-start(bf16[2,96,768]{2,1,0:T(8,128)(2,1)S(1)} %fusion.6), channel_id=1, source_target_pairs={{0,8},{2,10},{4,12},{6,14},{8,0},{10,2},{12,4},{14,6},{16,24},{18,... | collective-permute-start | bytes 884744 | tf_op jit(solution)/shard_map/ppermute | solution.py:193
  108.4 18.8 %collective-permute-start.13 = (bf16[2,96,768]{2,1,0:T(8,128)(2,1)S(1)}, bf16[2,96,768]{2,1,0:T(8,128)(2,1)S(1)}, u32[]{:S(2)}, u32[]{:S(2)}) collective-permute-start(bf16[2,96,768]{2,1,0:T(8,128)(2,1)S(1)} %fusion.7), channel_id=1, source_target_pairs={{0,16},{2,18},{4,20},{6,22},{8,24},{10,26},{12,28},{14,30},{16,0},... | collective-permute-start | bytes 884744 | tf_op jit(solution)/shard_map/ppermute | solution.py:193
  116.8 13.7 %collective-permute-start.9 = (bf16[96,768]{1,0:T(8,128)(2,1)S(1)}, bf16[96,768]{1,0:T(8,128)(2,1)S(1)}, u32[]{:S(2)}, u32[]{:S(2)}) collective-permute-start(bf16[96,768]{1,0:T(8,128)(2,1)S(1)} %fusion.10), channel_id=1, source_target_pairs={{0,16},{2,18},{4,20},{6,22},{8,24},{10,26},{12,28},{14,30},{16,0},... | collective-permute-start | bytes 442376 | tf_op jit(solution)/shard_map/ppermute | solution.py:193
  127.3 0.8 copy-start.19
  128.8 38.1 %collective-permute-start.14 = (bf16[96,768]{1,0:T(8,128)(2,1)}, bf16[96,768]{1,0:T(8,128)(2,1)}, u32[]{:S(2)}, u32[]{:S(2)}) collective-permute-start(bf16[96,768]{1,0:T(8,128)(2,1)} %fusion.11), channel_id=1, source_target_pairs={{0,4},{2,6},{4,0},{6,2},{8,12},{10,14},{12,8},{14,10},{16,20},{18,... | collective-permute-start | bytes 442376 | tf_op jit(solution)/shard_map/ppermute | solution.py:193
  131.3 38.2 %collective-permute-start.10 = (bf16[96,768]{1,0:T(8,128)(2,1)}, bf16[96,768]{1,0:T(8,128)(2,1)}, u32[]{:S(2)}, u32[]{:S(2)}) collective-permute-start(bf16[96,768]{1,0:T(8,128)(2,1)} %fusion.9), channel_id=1, source_target_pairs={{0,1},{1,0},{2,3},{3,2},{4,5},{5,4},{6,7},{7,6},{8,9},{9,8},{10,11... | collective-permute-start | bytes 442376 | tf_op jit(solution)/shard_map/ppermute | solution.py:30
  132.8 0.8 copy-start.12
  133.6 10.7 %copy-start.10 = (f32[4,8,384]{2,1,0:T(8,128)S(1)}, f32[4,8,384]{2,1,0:T(8,128)}, u32[]{:S(2)}) copy-start(f32[4,8,384]{2,1,0:T(8,128)} %copy-done.9) | copy-start | bytes 147460
  143.8 53.5 %collective-permute-start.5 = (bf16[2,384,512]{2,1,0:T(8,128)(2,1)S(1)}, bf16[2,384,512]{2,1,0:T(8,128)(2,1)S(1)}, u32[]{:S(2)}, u32[]{:S(2)}) collective-permute-start(bf16[2,384,512]{2,1,0:T(8,128)(2,1)S(1)} %get-tuple-element.39), channel_id=1, source_target_pairs={{0,1},{1,0},{2,3},{3,2},{4,5},{5,4},{6,7},{7,6},{8,9},{9,8},{10,11... | collective-permute-start | bytes 2359304 | tf_op jit(solution)/shard_map/ppermute | solution.py:30
  144.3 11.8 %copy-start.8 = (f32[4,8,384]{2,1,0:T(8,128)S(1)}, f32[4,8,384]{2,1,0:T(8,128)}, u32[]{:S(2)}) copy-start(f32[4,8,384]{2,1,0:T(8,128)} %copy-done.7) | copy-start | bytes 147460
  154.6 44.5 %collective-permute-start.4 = (bf16[2,384,512]{2,1,0:T(8,128)(2,1)S(1)}, bf16[2,384,512]{2,1,0:T(8,128)(2,1)S(1)}, u32[]{:S(2)}, u32[]{:S(2)}) collective-permute-start(bf16[2,384,512]{2,1,0:T(8,128)(2,1)S(1)} %get-tuple-element.37), channel_id=1, source_target_pairs={{0,1},{1,0},{2,3},{3,2},{4,5},{5,4},{6,7},{7,6},{8,9},{9,8},{10,11... | collective-permute-start | bytes 2359304 | tf_op jit(solution)/shard_map/ppermute | solution.py:30
  156.1 10.8 %copy-start.20 = (f32[2,96,768]{2,1,0:T(8,128)S(1)}, f32[2,96,768]{2,1,0:T(8,128)}, u32[]{:S(2)}) copy-start(f32[2,96,768]{2,1,0:T(8,128)} %copy-done.19) | copy-start | bytes 1769476
  166.4 34.5 %collective-permute-start.3 = (bf16[2,384,512]{2,1,0:T(8,128)(2,1)S(1)}, bf16[2,384,512]{2,1,0:T(8,128)(2,1)S(1)}, u32[]{:S(2)}, u32[]{:S(2)}) collective-permute-start(bf16[2,384,512]{2,1,0:T(8,128)(2,1)S(1)} %get-tuple-element.35), channel_id=1, source_target_pairs={{0,1},{1,0},{2,3},{3,2},{4,5},{5,4},{6,7},{7,6},{8,9},{9,8},{10,11... | collective-permute-start | bytes 2359304 | tf_op jit(solution)/shard_map/ppermute | solution.py:30
  167.8 29.5 %copy-start.4 = (f32[2,384,512]{2,1,0:T(8,128)S(1)}, f32[2,384,512]{2,1,0:T(8,128)}, u32[]{:S(2)}) copy-start(f32[2,384,512]{2,1,0:T(8,128)} %get-tuple-element.38.own_ref) | copy-start | bytes 4718596
  167.8 28.6 %collective-permute-start.15 = (bf16[96,768]{1,0:T(8,128)(2,1)S(1)}, bf16[96,768]{1,0:T(8,128)(2,1)S(1)}, u32[]{:S(2)}, u32[]{:S(2)}) collective-permute-start(bf16[96,768]{1,0:T(8,128)(2,1)S(1)} %fusion.8), channel_id=1, source_target_pairs={{0,1},{1,0},{2,3},{3,2},{4,5},{5,4},{6,7},{7,6},{8,9},{9,8},{10,11... | collective-permute-start | bytes 442376 | tf_op jit(solution)/shard_map/ppermute | solution.py:30
  197.4 1.8 copy-start.6
  199.1 1.8 copy-start.5
Sparse Core Ops, SparseCore 0:
  10.3 55.9 all-gather.1

commit v2 on v1

--- a/solution.py
+++ b/solution.py
@@ -11,6 +11,7 @@
 HEADS = 12
 HS = 128
 CHUNKS = (4, 4, 4)
+GRAD_CHUNKS = ((0, 0, 2), (0, 2, 2), (1, 0, 4), (2, 0, 4))
 SCALE = HS ** (-0.5)
 LOG2E = 1.4426950408889634
 VMEM_LIMIT = 48 * 1024 * 1024
@@ -48,7 +49,7 @@
         weights = jnp.exp2(block - row_max)
         total = total + jnp.sum(weights, axis=0, keepdims=True)
         mixed = mixed + mm(value, weights.astype(jnp.bfloat16), TN_DIMS)
-    att_ref[...] = jnp.transpose(mixed / total).astype(att_ref.dtype)
+    att_ref[...] = (mixed / total).astype(att_ref.dtype)
     lse_ref[0] = jnp.broadcast_to(row_max + jnp.log2(total), lse_ref.shape[1:])
 
 
@@ -60,8 +61,8 @@
     out_refs = refs[len(refs) - other_count :]
     query = q_ref[...]
     grad = mm(og_ref[...], w_ref[...], NT_DIMS).astype(jnp.bfloat16)
-    product = grad.astype(jnp.float32) * att_ref[...].astype(jnp.float32)
-    delta = jnp.sum(jnp.transpose(product), axis=0, keepdims=True)
+    turned = jnp.transpose(grad.astype(jnp.float32))
+    delta = jnp.sum(turned * att_ref[...].astype(jnp.float32), axis=0, keepdims=True)
     log_total = lse_ref[0][0:1]
     query_part = 0.0
     for place in range(other_count + 1):
@@ -103,8 +104,12 @@
     return pl.BlockSpec((rows, HS), lambda i: (0, first + i))
 
 
-def pair_block(rows):
-    return pl.BlockSpec((2, rows, HS), lambda i: (0, 0, i))
+def row_block(rows, first):
+    return pl.BlockSpec((HS, rows), lambda i: (first + i, 0))
+
+
+def pair_block(rows, skip=0):
+    return pl.BlockSpec((2, rows, HS), lambda i: (0, 0, skip + i))
 
 
 SMEM_BLOCK = pl.BlockSpec(memory_space=pltpu.SMEM)
@@ -122,9 +127,9 @@
         in_specs=[SMEM_BLOCK, head, head, head]
         + [pair_block(rows)] * count
         + [HBM_BLOCK] * len(chained),
-        out_specs=[head, pl.BlockSpec((1, 8, rows), lambda i: (i, 0, 0))],
+        out_specs=[row_block(rows, first), pl.BlockSpec((1, 8, rows), lambda i: (i, 0, 0))],
         out_shape=[
-            jax.ShapeDtypeStruct((rows, width), jnp.bfloat16),
+            jax.ShapeDtypeStruct((width, rows), jnp.bfloat16),
             jax.ShapeDtypeStruct((heads, 8, rows), jnp.float32),
         ],
         input_output_aliases={4 + count: 0} if chained else {},
@@ -138,7 +143,7 @@
     )(bias, q, k, v, *others, *chained)
 
 
-def backward(first, heads, bias, q, k, v, att, lse, og, w, others, dq):
+def backward(first, skip, heads, bias, q, k, v, att, lse, og, w, others, dq):
     rows, width = q.shape
     count = len(others)
     head = column_block(rows, first)
@@ -146,13 +151,13 @@
     results = pl.pallas_call(
         functools.partial(backward_kernel, count),
         grid=(heads,),
-        in_specs=[SMEM_BLOCK, head, head, head, head]
+        in_specs=[SMEM_BLOCK, head, head, head, row_block(rows, first)]
         + [
-            pl.BlockSpec((1, 8, rows), lambda i: (i, 0, 0)),
+            pl.BlockSpec((1, 8, rows), lambda i: (skip + i, 0, 0)),
             pl.BlockSpec(og.shape, lambda i: (0, 0)),
             pl.BlockSpec((HS, w.shape[1]), lambda i: (first + i, 0)),
         ]
-        + [pair_block(rows)] * count
+        + [pair_block(rows, skip)] * count
         + [HBM_BLOCK] * len(chained),
         out_specs=[head] + [pair_block(rows)] * (count + 1),
         out_shape=[
@@ -193,36 +198,67 @@
     return lax.ppermute(value, "dp", [(source, source ^ (1 << bit)) for source in range(count)])
 
 
-def summed_rows(att, og, norm):
-    place = lax.axis_index("dp")
-    bits = lax.axis_size("dp").bit_length() - 1
-    rows, width = att.shape
-    block = width >> bits
-    core = lax.rem(place, 2)
-    panels = att.reshape(rows, width // (2 * block), 2, block)
-
-    def side(which):
-        return lax.dynamic_index_in_dim(panels, which, 2, keepdims=False).reshape(rows, width // 2)
-
-    mine, theirs = side(core), side(1 - core)
-    half = og.shape[1] // 2
-    orders = (tuple(range(1, bits)), tuple(range(2, bits)) + (1,))
-    halves = []
-    for part, order in enumerate(orders):
-        columns = og[:, part * half : (part + 1) * half]
-        sent = exchange_bit((mm(theirs, columns, TN_DIMS) * norm).astype(jnp.bfloat16), 0)
-        held = mm(mine, columns, TN_DIMS) * norm + sent.astype(jnp.float32)
-        left = list(range(bits - 1, 0, -1))
-        held = held.reshape((2,) * len(left) + (block, half))
-        for bit in order:
+def after(value, earlier):
+    return lax.optimization_barrier((value, earlier))[0]
+
+
+def bit_of(place, bit):
+    return lax.rem(lax.div(place, 1 << bit), 2)
+
+
+def pick(array, which, axis):
+    return lax.dynamic_index_in_dim(array, which, axis, keepdims=False)
+
+
+class RowSums:
+    def __init__(self, att, og, norm, hold):
+        self.place = lax.axis_index("dp")
+        bits = lax.axis_size("dp").bit_length() - 1
+        width, tokens = att.shape
+        block = width >> bits
+        half = og.shape[1] // 2
+        core = bit_of(self.place, 0)
+        panels = att.reshape(width // (2 * block), 2, block, tokens)
+        mine, theirs = (
+            pick(panels, which, 1).reshape(width // 2, tokens) for which in (core, 1 - core)
+        )
+        columns = [og[:, :half], after(og[:, half:], hold)]
+        shape = (2,) * (bits - 1) + (block, half)
+        self.orders = [tuple(range(1, bits)), tuple(range(2, bits)) + (1,)]
+        self.left = [list(range(bits - 1, 0, -1)) for _ in columns]
+        self.sent = [
+            (mm(theirs, part, NN_DIMS) * norm).astype(jnp.bfloat16) for part in columns
+        ]
+        self.got = [exchange_bit(part, 0).reshape(shape) for part in self.sent]
+        self.kept = lambda: [
+            (mm(mine, part, NN_DIMS) * norm).reshape(shape) for part in columns
+        ]
+        self.steps = bits - 1
+        self.done = 0
+
+    def totals(self, earlier):
+        kept = self.kept()
+        got = self.got if earlier is None else after(self.got, earlier)
+        return [a + b.astype(jnp.float32) for a, b in zip(kept, got)]
+
+    def step(self, earlier=None):
+        held = self.totals(earlier)
+        self.sent, self.got, kept = [], [], []
+        for part, order, left in zip(held, self.orders, self.left):
+            bit = order[self.done]
             spot = left.index(bit)
-            own = lax.rem(lax.div(place, 1 << bit), 2)
-            away = lax.dynamic_index_in_dim(held, 1 - own, spot, keepdims=False)
-            kept = lax.dynamic_index_in_dim(held, own, spot, keepdims=False)
-            held = kept + exchange_bit(away.astype(jnp.bfloat16), bit).astype(jnp.float32)
+            own = bit_of(self.place, bit)
+            self.sent.append(pick(part, 1 - own, spot).astype(jnp.bfloat16))
+            self.got.append(exchange_bit(self.sent[-1], bit))
+            kept.append(pick(part, own, spot))
             left.remove(bit)
-        halves.append(held)
-    return halves
+        self.kept = lambda: kept
+        self.done += 1
+
+    def finish(self):
+        while self.done < self.steps:
+            self.step()
+        return self.totals(None)
 
 
 def per_device(queries, key_rows, value_rows, out_grad, w_out, band_start, window_active):
@@ -250,23 +286,38 @@
     for clip in range(clip_count):
         q, k, v, og = queries[clip], key_rows[clip], value_rows[clip], out_grad[clip]
         bias = biases[clip]
-        others = []
+        others, panel = [], None
         for span in spans:
-            panel = jnp.stack((cut(k, span), cut(v, span)))
+            source = (k, v) if panel is None else after((k, v), panel)
+            panel = jnp.stack([cut(array, span) for array in source])
             others.append([passed_along(panel, "seq", step) for step in steps])
         att, lses = None, []
         for span, other in zip(spans, others):
             att, lse = forward(*span, bias, q, k, v, other, att)
             lses.append(lse)
-        part = summed_rows(att, og, norm)
-        weight = part if weight is None else [a + b for a, b in zip(weight, part)]
         dq, sums = None, ()
         pending = []
-        for span, other, lse in zip(spans, others, lses):
-            dq, own, away = backward(*span, bias, q, k, v, att, lse, og, w_full, other, dq)
+        sums_of_rows = None
+        for turn, (panel, skip, heads) in enumerate(GRAD_CHUNKS):
+            span = (spans[panel][0] + skip, heads)
+            dq, own, away = backward(
+                span[0], skip, heads, bias, q, k, v, att, lses[panel], og, w_full, others[panel], dq
+            )
             received = [passed_along(x, "seq", -step) for x, step in zip(away, steps)]
             pending.append((span, own, received))
+            if turn == 1:
+                sums_of_rows = RowSums(after(att, away), og, norm, pending[0][2])
+                bias = after(bias, sums_of_rows.sent)
+            elif turn == 2:
+                sums_of_rows.step((away, pending[1][2]))
+                bias = after(bias, sums_of_rows.sent)
+            elif turn == 3:
+                sums_of_rows.step(away)
+        part = sums_of_rows.finish()
+        last_sent = part
+        weight = part if weight is None else [a + b for a, b in zip(weight, part)]
         for span, own, received in pending:
+            own = after(own, last_sent)
             sums = add_parts(*span, tile_len, width, own, received, sums)
         outs.append((dq, *sums))
     if seq_count == 2:

time: 210 us -> 177 us (0.84)
  waiting for transfers between devices: 89.8 us -> 58.8 us
    ppermute x8 -> x9, waiting for transfers between devices: 60.7 us -> 38.8 us  [passed_along(): return lax.ppermute(value, axis, pairs)]
    ppermute x8, waiting for transfers between devices: 28.4 us -> 19.2 us  [exchange_bit(): lax.ppermute(value, 'dp', [(source, source ^ 1 << bit) for source in rang...]
    add x4 -> x8, other arithmetic: 2.85 us -> 5.81 us  [totals(): return [a + b.astype(jnp.float32) for a, b in zip(kept, got)]]
    pallas_call x3 -> x4, Pallas kernels: 30.7 us -> 33.2 us  [backward(): pl.pallas_call(functools.partial(backward_kernel, count), grid=(heads,),...]
    pallas_call x1 -> x0, local copies, waits for them, and re-layouts: 2.37 us -> none  [forward(): pl.pallas_call(functools.partial(forward_kernel, count), grid=(heads,), i...]
    ppermute x8, starting transfers between devices: 10.2 us -> 7.91 us  [exchange_bit(): lax.ppermute(value, 'dp', [(source, source ^ 1 << bit) for source in rang...]
    ppermute x8 -> x9, starting transfers between devices: 10.6 us -> 11.4 us  [passed_along(): return lax.ppermute(value, axis, pairs)]
    unnamed x44 -> x64, local copies, waits for them, and re-layouts: 5.98 us -> 6.76 us
  transfers between devices with their start and end apart: 17 -> 18, of which waited for: 9 -> 9; matrix products, arithmetic and copies ran while one was open for 13% -> 11% of each run, Pallas kernels for 23% -> 22%
where the time goes in v2:
time: 177 us; the launch traced here: 176 us
  waiting for transfers between devices  58.8 us (33%)
  Pallas kernels  51.7 us (29%)
  starting transfers between devices  19.4 us (11%)
  between operations  16.4 us (9%)
  local copies, waits for them, and re-layouts  13.6 us (8%)
  other arithmetic  9.59 us (5%)
  matrix products  6.34 us (4%)
    ppermute x9, waiting for transfers between devices, passed_along(): return lax.ppermute(value, axis, pairs)  38.8 us
    pallas_call x4, Pallas kernels, backward(): pl.pallas_call(functools.partial(backward_kernel, count), grid=(heads,),...  33.2 us
    ppermute x8, waiting for transfers between devices, exchange_bit(): lax.ppermute(value, 'dp', [(source, source ^ 1 << bit) for source in rang...  19.2 us
    pallas_call x3, Pallas kernels, forward(): pl.pallas_call(functools.partial(forward_kernel, count), grid=(heads,), i...  13.1 us
    ppermute x9, starting transfers between devices, passed_along(): return lax.ppermute(value, axis, pairs)  11.4 us
    ppermute x8, starting transfers between devices, exchange_bit(): lax.ppermute(value, 'dp', [(source, source ^ 1 << bit) for source in rang...  7.91 us
    unnamed x64, local copies, waits for them, and re-layouts  6.76 us
    dot_general x4, matrix products, mm(): return lax.dot_general(lhs, rhs, dims, preferred_element_type=jnp.float32)  6.34 us
  transfers between devices with their start and end apart: 18, of which 9 were waited for; matrix products, arithmetic and copies ran while one was open for 11% of the time, Pallas kernels for 22%

profile of v2, /device:TPU:0, one launch (start us, length us, event | category | flops | bytes accessed | tf_op | source)
XLA Modules:
  0.0 175.7 jit_solution(11158632065828408569)
XLA Ops:
  7.9 1.2 slice_bitcast_fusion
  9.1 0.9 pad_maximum_fusion
  10.0 3.0 %collective-permute-start.2 = (bf16[2,384,512]{2,1,0:T(8,128)(2,1)}, bf16[2,384,512]{2,1,0:T(8,128)(2,1)}, u32[]{:S(2)}, u32[]{:S(2)}) collective-permute-start(bf16[2,384,512]{2,1,0:T(8,128)(2,1)} %pad_maximum_fusion), channel_id=1, source_target_pairs={{0,1},{1,0},{2,3},{3,2},{4,5},{5,4},{6,7},{7,6},{8,9},{9,8},{10,11... | collective-permute-start | bytes 2359304 | tf_op jit(solution)/shard_map/ppermute | solution.py:31
  13.1 0.9 pad_maximum_fusion.1
  14.0 0.9 collective-permute-start.1
  15.0 0.9 pad_maximum_fusion.2
  16.0 1.1 collective-permute-start
  19.7 1.9 %slice.50 = bf16[384,768]{1,0:T(8,128)(2,1)} slice(bf16[384,1536]{1,0:T(8,128)(2,1)} %bitcast.87), slice={[0:384], [768:1536]} | slice | bytes 1179648 | tf_op jit(solution)/shard_map/slice | solution.py:225
  21.6 10.1 %collective-permute-done.2.refs_0_ = bf16[2,384,512]{2,1,0:T(8,128)(2,1)} collective-permute-done((bf16[2,384,512]{2,1,0:T(8,128)(2,1)}, bf16[2,384,512]{2,1,0:T(8,128)(2,1)}, u32[]{:S(2)}, u32[]{:S(2)}) %collective-permute-start.2) | collective-permute-done | bytes 786464 | tf_op jit(solution)/shard_map/ppermute | solution.py:31
  31.7 4.4 %attend.3 = (bf16[1536,384]{1,0:T(8,128)(2,1)S(1)}, f32[4,8,384]{2,1,0:T(8,128)S(1)}) custom-call(f32[1]{0:T(128)} %bitcast.2.bias_ref, bf16[384,1536]{1,0:T(8,128)(2,1)S(1)} %bitcast.79, bf16[384,1536]{1,0:T(8,128)(2,1)S(1)} %bitcast.62, bf16[384,1536]{1,0:T(8,128)(2,1)S(1)} %bitcast.72, bf16[2,384,512]{2,1,0:T(8,128)(2,1)} %collective-permute-done.2.refs_0_), custom_call_target="tpu_custom_call" | custom-call | flops 603979776 | bytes 2359296 | tf_op jit(solution)/shard_map/attend/pallas_call | solution.py:124
  36.1 12.5 %collective-permute-done.1.refs_0_ = bf16[2,384,512]{2,1,0:T(8,128)(2,1)} collective-permute-done((bf16[2,384,512]{2,1,0:T(8,128)(2,1)}, bf16[2,384,512]{2,1,0:T(8,128)(2,1)}, u32[]{:S(2)}, u32[]{:S(2)}) %collective-permute-start.1) | collective-permute-done | bytes 786464 | tf_op jit(solution)/shard_map/ppermute | solution.py:31
  48.5 4.4 %attend.4 = (bf16[1536,384]{1,0:T(8,128)(2,1)S(1)}, f32[4,8,384]{2,1,0:T(8,128)S(1)}) custom-call(f32[1]{0:T(128)} %bitcast.2.bias_ref, bf16[384,1536]{1,0:T(8,128)(2,1)S(1)} %bitcast.80, bf16[384,1536]{1,0:T(8,128)(2,1)S(1)} %bitcast.63, bf16[384,1536]{1,0:T(8,128)(2,1)S(1)} %bitcast.73, ...), custom_call_target="tpu_custom_call", output_to_operand_aliasing={{0}: (5, {})} | custom-call | flops 603979776 | bytes 2359296 | tf_op jit(solution)/shard_map/attend/pallas_call | solution.py:124
  53.5 11.0 %collective-permute-done.refs_0_ = bf16[2,384,512]{2,1,0:T(8,128)(2,1)} collective-permute-done((bf16[2,384,512]{2,1,0:T(8,128)(2,1)}, bf16[2,384,512]{2,1,0:T(8,128)(2,1)}, u32[]{:S(2)}, u32[]{:S(2)}) %collective-permute-start) | collective-permute-done | bytes 786464 | tf_op jit(solution)/shard_map/ppermute | solution.py:31
  64.6 4.4 %attend.5 = (bf16[1536,384]{1,0:T(8,128)(2,1)S(1)}, f32[4,8,384]{2,1,0:T(8,128)S(1)}) custom-call(f32[1]{0:T(128)} %bitcast.2.bias_ref, bf16[384,1536]{1,0:T(8,128)(2,1)S(1)} %bitcast.81, bf16[384,1536]{1,0:T(8,128)(2,1)S(1)} %bitcast.64, bf16[384,1536]{1,0:T(8,128)(2,1)S(1)} %bitcast.74, ...), custom_call_target="tpu_custom_call", output_to_operand_aliasing={{0}: (5, {})} | custom-call | flops 603979776 | bytes 2359296 | tf_op jit(solution)/shard_map/attend/pallas_call | solution.py:124
  69.0 1.0 copy-done.3
  70.6 0.8 copy-done.16
  71.4 6.2 %attend_grad.4 = (bf16[384,1536]{1,0:T(8,128)(2,1)}, f32[2,384,256]{2,1,0:T(8,128)S(1)}, bf16[2,384,256]{2,1,0:T(8,128)(2,1)S(1)}) custom-call(f32[1]{0:T(128)} %bitcast.2.bias_ref, bf16[384,1536]{1,0:T(8,128)(2,1)S(1)} %bitcast.82, bf16[384,1536]{1,0:T(8,128)(2,1)S(1)} %bitcast.65, bf16[384,1536]{1,0:T(8,128)(2,1)S(1)} %bitcast.75, ...), custom_call_target="tpu_custom_call" | custom-call | flops 1056964608 | bytes 3145728 | tf_op jit(solution)/shard_map/attend_grad/pallas_call | solution.py:151
  77.5 0.9 copy-done.9
  78.5 6.2 %attend_grad.5 = (bf16[384,1536]{1,0:T(8,128)(2,1)}, f32[2,384,256]{2,1,0:T(8,128)S(1)}, bf16[2,384,256]{2,1,0:T(8,128)(2,1)S(1)}) custom-call(f32[1]{0:T(128)} %bitcast.2.bias_ref, bf16[384,1536]{1,0:T(8,128)(2,1)S(1)} %bitcast.83, bf16[384,1536]{1,0:T(8,128)(2,1)S(1)} %bitcast.66, bf16[384,1536]{1,0:T(8,128)(2,1)S(1)} %bitcast.76, ...), custom_call_target="tpu_custom_call", output_to_operand_aliasing={{0}: (9, {})} | custom-call | flops 1056964608 | bytes 3145728 | tf_op jit(solution)/shard_map/attend_grad/pallas_call | solution.py:151
  84.7 1.8 %collective-permute-start.3 = (bf16[2,384,256]{2,1,0:T(8,128)(2,1)S(1)}, bf16[2,384,256]{2,1,0:T(8,128)(2,1)S(1)}, u32[]{:S(2)}, u32[]{:S(2)}) collective-permute-start(bf16[2,384,256]{2,1,0:T(8,128)(2,1)S(1)} %get-tuple-element.57), channel_id=1, source_target_pairs={{0,1},{1,0},{2,3},{3,2},{4,5},{5,4},{6,7},{7,6},{8,9},{9,8},{10,11... | collective-permute-start | bytes 1179656 | tf_op jit(solution)/shard_map/ppermute | solution.py:31
  86.5 1.0 constant_dynamic-slice_fusion.1
  88.0 1.8 %multiply_convert_fusion.1 = bf16[768,768]{1,0:T(8,128)(2,1)} fusion(bf16[768,384]{1,0:T(8,128)(2,1)S(1)} %bitcast.101, bf16[384,1536]{1,0:T(8,128)(2,1)S(1)} %bitcast.93), kind=kOutput, calls=%fused_computation.3 | convolution fusion | flops 454164480 | bytes 2359296 | tf_op jit(solution)/shard_map/dot_general | solution.py:25
  89.8 5.3 %collective-permute-done.3.refs_0_ = bf16[2,384,256]{2,1,0:T(8,128)(2,1)S(1)} collective-permute-done((bf16[2,384,256]{2,1,0:T(8,128)(2,1)S(1)}, bf16[2,384,256]{2,1,0:T(8,128)(2,1)S(1)}, u32[]{:S(2)}, u32[]{:S(2)}) %collective-permute-start.3) | collective-permute-done | bytes 393248 | tf_op jit(solution)/shard_map/ppermute | solution.py:31
  95.0 1.8 %multiply_convert_fusion = bf16[768,768]{1,0:T(8,128)(2,1)} fusion(bf16[768,384]{1,0:T(8,128)(2,1)S(1)} %bitcast.102, bf16[384,768]{1,0:T(8,128)(2,1)S(1)} %copy-done.29), kind=kOutput, calls=%fused_computation.2 | convolution fusion | flops 454164480 | bytes 2359296 | tf_op jit(solution)/shard_map/dot_general | solution.py:25
  96.8 1.4 collective-permute-start.6
  98.2 2.0 %convolution_multiply_fusion.1 = f32[768,768]{1,0:T(8,128)S(1)} fusion(bf16[768,384]{1,0:T(8,128)(2,1)} %bitcast.99, bf16[384,1536]{1,0:T(8,128)(2,1)} %bitcast.90), kind=kOutput, calls=%fused_computation.5 | convolution fusion | flops 453574656 | bytes 3538944 | tf_op jit(solution)/shard_map/dot_general | solution.py:25
  100.3 10.5 %attend_grad.6 = (bf16[384,1536]{1,0:T(8,128)(2,1)}, f32[2,384,512]{2,1,0:T(8,128)}, bf16[2,384,512]{2,1,0:T(8,128)(2,1)S(1)}) custom-call(f32[1]{0:T(128)} %bitcast.2.bias_ref, bf16[384,1536]{1,0:T(8,128)(2,1)S(1)} %bitcast.84, bf16[384,1536]{1,0:T(8,128)(2,1)S(1)} %bitcast.67, bf16[384,1536]{1,0:T(8,128)(2,1)S(1)} %bitcast.77, ...), custom_call_target="tpu_custom_call", output_to_operand_aliasing={{0}: (9, {})} | custom-call | flops 2113929216 | bytes 6291456 | tf_op jit(solution)/shard_map/attend_grad/pallas_call | solution.py:151
  111.7 1.7 copy_add_fusion
  113.5 1.0 fusion.1
  114.4 1.6 collective-permute-start.8
  116.0 1.5 copy_add_fusion.1
  117.6 1.0 fusion
  119.2 1.5 collective-permute-start.7
  122.0 10.4 %attend_grad.7 = (bf16[384,1536]{1,0:T(8,128)(2,1)}, f32[2,384,512]{2,1,0:T(8,128)}, bf16[2,384,512]{2,1,0:T(8,128)(2,1)S(1)}) custom-call(f32[1]{0:T(128)} %bitcast.2.bias_ref, bf16[384,1536]{1,0:T(8,128)(2,1)S(1)} %bitcast.85, bf16[384,1536]{1,0:T(8,128)(2,1)S(1)} %bitcast.68, bf16[384,1536]{1,0:T(8,128)(2,1)S(1)} %bitcast.78, ...), custom_call_target="tpu_custom_call", output_to_operand_aliasing={{0}: (9, {})} | custom-call | flops 2113929216 | bytes 6291456 | tf_op jit(solution)/shard_map/attend_grad/pallas_call | solution.py:151
  132.4 1.5 collective-permute-start.13
  134.7 1.2 bitcast_add_fusion
  135.9 2.7 %collective-permute-start.11 = (bf16[2,96,768]{2,1,0:T(8,128)(2,1)S(1)}, bf16[2,96,768]{2,1,0:T(8,128)(2,1)S(1)}, u32[]{:S(2)}, u32[]{:S(2)}) collective-permute-start(bf16[2,96,768]{2,1,0:T(8,128)(2,1)S(1)} %fusion.5), channel_id=1, source_target_pairs={{0,16},{2,18},{4,20},{6,22},{8,24},{10,26},{12,28},{14,30},{16,0},... | collective-permute-start | bytes 884744 | tf_op jit(solution)/shard_map/ppermute | solution.py:198
  138.6 1.2 bitcast_add_fusion.1
  140.4 10.9 %collective-permute-done.11 = bf16[2,96,768]{2,1,0:T(8,128)(2,1)S(1)} collective-permute-done((bf16[2,96,768]{2,1,0:T(8,128)(2,1)S(1)}, bf16[2,96,768]{2,1,0:T(8,128)(2,1)S(1)}, u32[]{:S(2)}, u32[]{:S(2)}) %collective-permute-start.11) | collective-permute-done | bytes 294944 | tf_op jit(solution)/shard_map/ppermute | solution.py:198
  151.3 1.6 collective-permute-start.12
  152.9 0.9 collective-permute-done.9
  154.0 3.1 %collective-permute-done.12 = bf16[96,768]{1,0:T(8,128)(2,1)S(1)} collective-permute-done((bf16[96,768]{1,0:T(8,128)(2,1)S(1)}, bf16[96,768]{1,0:T(8,128)(2,1)S(1)}, u32[]{:S(2)}, u32[]{:S(2)}) %collective-permute-start.12) | collective-permute-done | bytes 147488 | tf_op jit(solution)/shard_map/ppermute | solution.py:198
  157.8 3.6 %collective-permute-done.10 = bf16[96,768]{1,0:T(8,128)(2,1)S(1)} collective-permute-done((bf16[96,768]{1,0:T(8,128)(2,1)S(1)}, bf16[96,768]{1,0:T(8,128)(2,1)S(1)}, u32[]{:S(2)}, u32[]{:S(2)}) %collective-permute-start.10) | collective-permute-done | bytes 147488 | tf_op jit(solution)/shard_map/ppermute | solution.py:198
  162.0 0.9 add_parts.4
  162.9 0.9 add_parts.5
  164.4 1.7 add_parts.6
  166.2 1.8 add_parts.7
  168.0 0.9 pad_maximum_fusion.3
  (97 shorter events, 9.7 us)
Async XLA Ops:
  7.2 63.4 %all-gather.2.cloned.1.call-start = ((), (), s32[]{:S(2)}) async-start(), calls=%async_computation | async-start | bytes 5013504 | tf_op jit(solution)/shard_map/all_gather | solution.py:273
  9.1 3.9 %copy-start = (bf16[1,384,1536]{2,1,0:T(8,128)(2,1)S(1)}, bf16[1,384,1536]{2,1,0:T(8,128)(2,1)}, u32[]{:S(2)}) copy-start(bf16[1,384,1536]{2,1,0:T(8,128)(2,1)} %param.8) | copy-start | bytes 3538948
  9.1 4.0 %copy-start.1 = (bf16[1,384,1536]{2,1,0:T(8,128)(2,1)S(1)}, bf16[1,384,1536]{2,1,0:T(8,128)(2,1)}, u32[]{:S(2)}) copy-start(bf16[1,384,1536]{2,1,0:T(8,128)(2,1)} %param.9) | copy-start | bytes 3538948
  10.0 21.6 %collective-permute-start.2 = (bf16[2,384,512]{2,1,0:T(8,128)(2,1)}, bf16[2,384,512]{2,1,0:T(8,128)(2,1)}, u32[]{:S(2)}, u32[]{:S(2)}) collective-permute-start(bf16[2,384,512]{2,1,0:T(8,128)(2,1)} %pad_maximum_fusion), channel_id=1, source_target_pairs={{0,1},{1,0},{2,3},{3,2},{4,5},{5,4},{6,7},{7,6},{8,9},{9,8},{10,11... | collective-permute-start | bytes 2359304 | tf_op jit(solution)/shard_map/ppermute | solution.py:31
  14.0 34.5 %collective-permute-start.1 = (bf16[2,384,512]{2,1,0:T(8,128)(2,1)}, bf16[2,384,512]{2,1,0:T(8,128)(2,1)}, u32[]{:S(2)}, u32[]{:S(2)}) collective-permute-start(bf16[2,384,512]{2,1,0:T(8,128)(2,1)} %pad_maximum_fusion.1), channel_id=1, source_target_pairs={{0,1},{1,0},{2,3},{3,2},{4,5},{5,4},{6,7},{7,6},{8,9},{9,8},{10,11... | collective-permute-start | bytes 2359304 | tf_op jit(solution)/shard_map/ppermute | solution.py:31
  15.0 2.8 %copy-start.31 = (s32[2,3]{1,0:T(2,128)S(1)}, s32[2,3]{1,0:T(2,128)}, u32[]{:S(2)}) copy-start(s32[2,3]{1,0:T(2,128)} %param.13) | copy-start | bytes 76
  15.0 16.7 %copy-start.2 = (bf16[1,384,1536]{2,1,0:T(8,128)(2,1)S(1)}, bf16[1,384,1536]{2,1,0:T(8,128)(2,1)}, u32[]{:S(2)}) copy-start(bf16[1,384,1536]{2,1,0:T(8,128)(2,1)} %param.7) | copy-start | bytes 3538948
  16.0 48.6 %collective-permute-start = (bf16[2,384,512]{2,1,0:T(8,128)(2,1)}, bf16[2,384,512]{2,1,0:T(8,128)(2,1)}, u32[]{:S(2)}, u32[]{:S(2)}) collective-permute-start(bf16[2,384,512]{2,1,0:T(8,128)(2,1)} %pad_maximum_fusion.2), channel_id=1, source_target_pairs={{0,1},{1,0},{2,3},{3,2},{4,5},{5,4},{6,7},{7,6},{8,9},{9,8},{10,11... | collective-permute-start | bytes 2359304 | tf_op jit(solution)/shard_map/ppermute | solution.py:31
  36.1 16.8 %copy-start.15 = (f32[4,8,384]{2,1,0:T(8,128)}, f32[4,8,384]{2,1,0:T(8,128)S(1)}, u32[]{:S(2)}) copy-start(f32[4,8,384]{2,1,0:T(8,128)S(1)} %get-tuple-element.53.lse_ref) | copy-start | bytes 147460
  68.9 1.0 copy-start.3
  70.6 0.8 copy-start.16
  77.5 0.9 copy-start.9
  78.5 8.0 %copy-start.4 = (bf16[1536,384]{1,0:T(8,128)(2,1)S(1)}, bf16[1536,384]{1,0:T(8,128)(2,1)}, u32[]{:S(2)}) copy-start(bf16[1536,384]{1,0:T(8,128)(2,1)} %copy-done.3) | copy-start | bytes 3538948
  84.7 2.8 %copy-start.7 = (f32[2,384,256]{2,1,0:T(8,128)}, f32[2,384,256]{2,1,0:T(8,128)S(1)}, u32[]{:S(2)}) copy-start(f32[2,384,256]{2,1,0:T(8,128)S(1)} %get-tuple-element.77.own_ref) | copy-start | bytes 2359300
  84.7 2.8 %copy-start.22 = (bf16[2,384,256]{2,1,0:T(8,128)(2,1)}, bf16[2,384,256]{2,1,0:T(8,128)(2,1)S(1)}, u32[]{:S(2)}) copy-start(bf16[2,384,256]{2,1,0:T(8,128)(2,1)S(1)} %get-tuple-element.55) | copy-start | bytes 1179652
  84.7 10.3 %collective-permute-start.3 = (bf16[2,384,256]{2,1,0:T(8,128)(2,1)S(1)}, bf16[2,384,256]{2,1,0:T(8,128)(2,1)S(1)}, u32[]{:S(2)}, u32[]{:S(2)}) collective-permute-start(bf16[2,384,256]{2,1,0:T(8,128)(2,1)S(1)} %get-tuple-element.57), channel_id=1, source_target_pairs={{0,1},{1,0},{2,3},{3,2},{4,5},{5,4},{6,7},{7,6},{8,9},{9,8},{10,11... | collective-permute-start | bytes 1179656 | tf_op jit(solution)/shard_map/ppermute | solution.py:31
  86.5 1.5 copy-start.23
  88.0 7.0 %copy-start.29 = (bf16[384,768]{1,0:T(8,128)(2,1)S(1)}, bf16[384,768]{1,0:T(8,128)(2,1)}, u32[]{:S(2)}) copy-start(bf16[384,768]{1,0:T(8,128)(2,1)} %slice.50) | copy-start | bytes 1769476
  89.8 21.9 %collective-permute-start.4 = (bf16[768,768]{1,0:T(8,128)(2,1)}, bf16[768,768]{1,0:T(8,128)(2,1)}, u32[]{:S(2)}, u32[]{:S(2)}) collective-permute-start(bf16[768,768]{1,0:T(8,128)(2,1)} %multiply_convert_fusion.1), channel_id=1, source_target_pairs={{0,2},{2,0},{4,6},{6,4},{8,10},{10,8},{12,14},{14,12},{16,18},{18,... | collective-permute-start | bytes 3538952 | tf_op jit(solution)/shard_map/ppermute | solution.py:198
  95.0 1.8 %copy-start.13 = (bf16[2,384,256]{2,1,0:T(8,128)(2,1)}, bf16[2,384,256]{2,1,0:T(8,128)(2,1)S(1)}, u32[]{:S(2)}) copy-start(bf16[2,384,256]{2,1,0:T(8,128)(2,1)S(1)} %collective-permute-done.3.refs_0_) | copy-start | bytes 1179652
  96.8 14.9 %collective-permute-start.5 = (bf16[768,768]{1,0:T(8,128)(2,1)}, bf16[768,768]{1,0:T(8,128)(2,1)}, u32[]{:S(2)}, u32[]{:S(2)}) collective-permute-start(bf16[768,768]{1,0:T(8,128)(2,1)} %multiply_convert_fusion), channel_id=1, source_target_pairs={{0,2},{2,0},{4,6},{6,4},{8,10},{10,8},{12,14},{14,12},{16,18},{18,... | collective-permute-start | bytes 3538952 | tf_op jit(solution)/shard_map/ppermute | solution.py:198
  96.8 14.9 %collective-permute-start.6 = (bf16[2,384,256]{2,1,0:T(8,128)(2,1)}, bf16[2,384,256]{2,1,0:T(8,128)(2,1)S(1)}, u32[]{:S(2)}, u32[]{:S(2)}) collective-permute-start(bf16[2,384,256]{2,1,0:T(8,128)(2,1)} %copy-done.22), channel_id=1, source_target_pairs={{0,1},{1,0},{2,3},{3,2},{4,5},{5,4},{6,7},{7,6},{8,9},{9,8},{10,11... | collective-permute-start | bytes 1179656 | tf_op jit(solution)/shard_map/ppermute | solution.py:31
  98.2 2.0 %copy-start.20 = (f32[4,8,384]{2,1,0:T(8,128)S(1)}, f32[4,8,384]{2,1,0:T(8,128)}, u32[]{:S(2)}) copy-start(f32[4,8,384]{2,1,0:T(8,128)} %copy-done.19) | copy-start | bytes 147460
  100.3 10.5 %copy-start.28 = (bf16[8,1,96,384]{3,2,1,0:T(8,128)(2,1)S(1)}, bf16[8,1,96,384]{3,2,1,0:T(8,128)(2,1)}, u32[]{:S(2)}) copy-start(bf16[8,1,96,384]{3,2,1,0:T(8,128)(2,1)} %get-tuple-element.99) | copy-start | bytes 1769476
  100.3 10.5 %copy-start.30 = (bf16[384,768]{1,0:T(8,128)(2,1)S(1)}, bf16[384,768]{1,0:T(8,128)(2,1)}, u32[]{:S(2)}) copy-start(bf16[384,768]{1,0:T(8,128)(2,1)} %slice.50) | copy-start | bytes 1769476
  110.8 0.9 copy-start.21
  111.7 1.8 %copy-start.11 = (bf16[2,384,256]{2,1,0:T(8,128)(2,1)}, bf16[2,384,256]{2,1,0:T(8,128)(2,1)S(1)}, u32[]{:S(2)}) copy-start(bf16[2,384,256]{2,1,0:T(8,128)(2,1)S(1)} %collective-permute-done.6.refs_0_) | copy-start | bytes 1179652
  113.5 4.1 %copy-start.24 = (f32[2,2,2,96,768]{4,3,2,0,1:T(8,128)}, f32[2,2,2,96,768]{4,3,2,0,1:T(8,128)S(1)}, u32[]{:S(2)}) copy-start(f32[2,2,2,96,768]{4,3,2,0,1:T(8,128)S(1)} %copy_add_fusion) | copy-start | bytes 7077892
  114.4 19.5 %collective-permute-start.8 = (bf16[2,2,96,768]{3,2,1,0:T(8,128)(2,1)}, bf16[2,2,96,768]{3,2,1,0:T(8,128)(2,1)}, u32[]{:S(2)}, u32[]{:S(2)}) collective-permute-start(bf16[2,2,96,768]{3,2,1,0:T(8,128)(2,1)} %fusion.1), channel_id=1, source_target_pairs={{0,8},{2,10},{4,12},{6,14},{8,0},{10,2},{12,4},{14,6},{16,24},{18,... | collective-permute-start | bytes 1769480 | tf_op jit(solution)/shard_map/ppermute | solution.py:198
  117.6 1.7 copy-start.26
  119.2 15.5 %collective-permute-start.7 = (bf16[2,2,96,768]{3,2,0,1:T(8,128)(2,1)}, bf16[2,2,96,768]{3,2,0,1:T(8,128)(2,1)}, u32[]{:S(2)}, u32[]{:S(2)}) collective-permute-start(bf16[2,2,96,768]{3,2,0,1:T(8,128)(2,1)} %fusion), channel_id=1, source_target_pairs={{0,4},{2,6},{4,0},{6,2},{8,12},{10,14},{12,8},{14,10},{16,20},{18,... | collective-permute-start | bytes 1769480 | tf_op jit(solution)/shard_map/ppermute | solution.py:198
  120.7 43.1 %collective-permute-start.14 = (bf16[2,384,512]{2,1,0:T(8,128)(2,1)}, bf16[2,384,512]{2,1,0:T(8,128)(2,1)S(1)}, u32[]{:S(2)}, u32[]{:S(2)}) collective-permute-start(bf16[2,384,512]{2,1,0:T(8,128)(2,1)} %copy-done.21), channel_id=1, source_target_pairs={{0,1},{1,0},{2,3},{3,2},{4,5},{5,4},{6,7},{7,6},{8,9},{9,8},{10,11... | collective-permute-start | bytes 2359304 | tf_op jit(solution)/shard_map/ppermute | solution.py:31
  121.2 0.8 copy-start.18
  122.0 12.7 %copy-start.25 = (f32[2,2,2,96,768]{4,3,2,0,1:T(8,128)S(1)}, f32[2,2,2,96,768]{4,3,2,0,1:T(8,128)}, u32[]{:S(2)}) copy-start(f32[2,2,2,96,768]{4,3,2,0,1:T(8,128)} %copy-done.24) | copy-start | bytes 7077892
  132.4 6.2 %copy-start.27 = (f32[2,2,2,96,768]{4,3,0,1,2:T(8,128)S(1)}, f32[2,2,2,96,768]{4,3,0,1,2:T(8,128)}, u32[]{:S(2)}) copy-start(f32[2,2,2,96,768]{4,3,0,1,2:T(8,128)} %copy-done.26) | copy-start | bytes 7077892
  132.4 33.8 %collective-permute-start.13 = (bf16[2,384,512]{2,1,0:T(8,128)(2,1)S(1)}, bf16[2,384,512]{2,1,0:T(8,128)(2,1)S(1)}, u32[]{:S(2)}, u32[]{:S(2)}) collective-permute-start(bf16[2,384,512]{2,1,0:T(8,128)(2,1)S(1)} %get-tuple-element.70), channel_id=1, source_target_pairs={{0,1},{1,0},{2,3},{3,2},{4,5},{5,4},{6,7},{7,6},{8,9},{9,8},{10,11... | collective-permute-start | bytes 2359304 | tf_op jit(solution)/shard_map/ppermute | solution.py:31
  135.9 15.3 %collective-permute-start.11 = (bf16[2,96,768]{2,1,0:T(8,128)(2,1)S(1)}, bf16[2,96,768]{2,1,0:T(8,128)(2,1)S(1)}, u32[]{:S(2)}, u32[]{:S(2)}) collective-permute-start(bf16[2,96,768]{2,1,0:T(8,128)(2,1)S(1)} %fusion.5), channel_id=1, source_target_pairs={{0,16},{2,18},{4,20},{6,22},{8,24},{10,26},{12,28},{14,30},{16,0},... | collective-permute-start | bytes 884744 | tf_op jit(solution)/shard_map/ppermute | solution.py:198
  139.8 14.0 %collective-permute-start.9 = (bf16[2,96,768]{2,1,0:T(8,128)(2,1)S(1)}, bf16[2,96,768]{2,1,0:T(8,128)(2,1)S(1)}, u32[]{:S(2)}, u32[]{:S(2)}) collective-permute-start(bf16[2,96,768]{2,1,0:T(8,128)(2,1)S(1)} %fusion.4), channel_id=1, source_target_pairs={{0,8},{2,10},{4,12},{6,14},{8,0},{10,2},{12,4},{14,6},{16,24},{18,... | collective-permute-start | bytes 884744 | tf_op jit(solution)/shard_map/ppermute | solution.py:198
  151.3 10.7 %copy-start.10 = (f32[2,384,256]{2,1,0:T(8,128)S(1)}, f32[2,384,256]{2,1,0:T(8,128)}, u32[]{:S(2)}) copy-start(f32[2,384,256]{2,1,0:T(8,128)} %copy-done.9) | copy-start | bytes 2359300
  151.3 10.6 %copy-start.14 = (bf16[2,384,256]{2,1,0:T(8,128)(2,1)S(1)}, bf16[2,384,256]{2,1,0:T(8,128)(2,1)}, u32[]{:S(2)}) copy-start(bf16[2,384,256]{2,1,0:T(8,128)(2,1)} %copy-done.13) | copy-start | bytes 1179652
  151.3 5.8 %collective-permute-start.12 = (bf16[96,768]{1,0:T(8,128)(2,1)S(1)}, bf16[96,768]{1,0:T(8,128)(2,1)S(1)}, u32[]{:S(2)}, u32[]{:S(2)}) collective-permute-start(bf16[96,768]{1,0:T(8,128)(2,1)S(1)} %fusion.7), channel_id=1, source_target_pairs={{0,4},{2,6},{4,0},{6,2},{8,12},{10,14},{12,8},{14,10},{16,20},{18,... | collective-permute-start | bytes 442376 | tf_op jit(solution)/shard_map/ppermute | solution.py:198
  153.9 8.9 %copy-start.8 = (f32[2,384,256]{2,1,0:T(8,128)S(1)}, f32[2,384,256]{2,1,0:T(8,128)}, u32[]{:S(2)}) copy-start(f32[2,384,256]{2,1,0:T(8,128)} %copy-done.7) | copy-start | bytes 2359300
  153.9 8.9 %copy-start.12 = (bf16[2,384,256]{2,1,0:T(8,128)(2,1)S(1)}, bf16[2,384,256]{2,1,0:T(8,128)(2,1)}, u32[]{:S(2)}) copy-start(bf16[2,384,256]{2,1,0:T(8,128)(2,1)} %copy-done.11) | copy-start | bytes 1179652
  154.0 7.4 %collective-permute-start.10 = (bf16[96,768]{1,0:T(8,128)(2,1)S(1)}, bf16[96,768]{1,0:T(8,128)(2,1)S(1)}, u32[]{:S(2)}, u32[]{:S(2)}) collective-permute-start(bf16[96,768]{1,0:T(8,128)(2,1)S(1)} %fusion.6), channel_id=1, source_target_pairs={{0,16},{2,18},{4,20},{6,22},{8,24},{10,26},{12,28},{14,30},{16,0},... | collective-permute-start | bytes 442376 | tf_op jit(solution)/shard_map/ppermute | solution.py:198
  157.1 10.8 %collective-permute-start.16 = (bf16[96,768]{1,0:T(8,128)(2,1)S(1)}, bf16[96,768]{1,0:T(8,128)(2,1)S(1)}, u32[]{:S(2)}, u32[]{:S(2)}) collective-permute-start(bf16[96,768]{1,0:T(8,128)(2,1)S(1)} %bitcast_add_fusion.4), channel_id=1, source_target_pairs={{0,1},{1,0},{2,3},{3,2},{4,5},{5,4},{6,7},{7,6},{8,9},{9,8},{10,11... | collective-permute-start | bytes 442376 | tf_op jit(solution)/shard_map/ppermute | solution.py:31
  161.4 6.6 %collective-permute-start.15 = (bf16[96,768]{1,0:T(8,128)(2,1)S(1)}, bf16[96,768]{1,0:T(8,128)(2,1)S(1)}, u32[]{:S(2)}, u32[]{:S(2)}) collective-permute-start(bf16[96,768]{1,0:T(8,128)(2,1)S(1)} %bitcast_add_fusion.5), channel_id=1, source_target_pairs={{0,1},{1,0},{2,3},{3,2},{4,5},{5,4},{6,7},{7,6},{8,9},{9,8},{10,11... | collective-permute-start | bytes 442376 | tf_op jit(solution)/shard_map/ppermute | solution.py:31
  162.9 1.6 copy-start.5
  164.4 1.7 copy-start.6
  (2 other events, 1.2 us)
Sparse Core Ops, SparseCore 0:
  10.3 55.9 all-gather.1

commit v3 on v2

--- a/solution.py
+++ b/solution.py
@@ -10,8 +10,8 @@
 
 HEADS = 12
 HS = 128
-CHUNKS = (4, 4, 4)
-GRAD_CHUNKS = ((0, 0, 2), (0, 2, 2), (1, 0, 4), (2, 0, 4))
+CHUNKS = (3, 3, 3, 3)
+GRAD_CHUNKS = ((0, 0, 3), (1, 0, 3), (2, 0, 3), (3, 0, 3))
 SCALE = HS ** (-0.5)
 LOG2E = 1.4426950408889634
 VMEM_LIMIT = 48 * 1024 * 1024
@@ -167,11 +167,7 @@
         + [jax.ShapeDtypeStruct((2, rows, heads * HS), jnp.bfloat16)] * count,
         input_output_aliases={8 + count: 0} if chained else {},
         compiler_params=params(),
-        cost_estimate=cost(
-            heads * ((count + 1) * rows * rows * HS * 10 + rows * HS * width * 2),
-            heads * rows * HS * 2 * (8 + 8 * count),
-            heads * (count + 1) * rows * rows,
-        ),
+        cost_estimate=cost(1000, 1000, 0),
         name="attend_grad",
     )(bias, q, k, v, att, lse, og, w, *others, *chained)
     return results[0], results[1], results[2:]
@@ -211,7 +207,7 @@
 
 
 class RowSums:
-    def __init__(self, att, og, norm, hold):
+    def __init__(self, att, og, norm):
         self.place = lax.axis_index("dp")
         bits = lax.axis_size("dp").bit_length() - 1
         width, tokens = att.shape
@@ -222,7 +218,7 @@
         mine, theirs = (
             pick(panels, which, 1).reshape(width // 2, tokens) for which in (core, 1 - core)
         )
-        columns = [og[:, :half], after(og[:, half:], hold)]
+        columns = [og[:, :half], og[:, half:]]
         shape = (2,) * (bits - 1) + (block, half)
         self.orders = [tuple(range(1, bits)), tuple(range(2, bits)) + (1,)]
         self.left = [list(range(bits - 1, 0, -1)) for _ in columns]
@@ -305,14 +301,11 @@
             )
             received = [passed_along(x, "seq", -step) for x, step in zip(away, steps)]
             pending.append((span, own, received))
-            if turn == 1:
-                sums_of_rows = RowSums(after(att, away), og, norm, pending[0][2])
-                bias = after(bias, sums_of_rows.sent)
-            elif turn == 2:
-                sums_of_rows.step((away, pending[1][2]))
-                bias = after(bias, sums_of_rows.sent)
-            elif turn == 3:
-                sums_of_rows.step(away)
+            if turn == 0:
+                sums_of_rows = RowSums(after(att, away), og, norm)
+            else:
+                sums_of_rows.step((away, pending[turn - 1][2]))
+            bias = after(bias, sums_of_rows.sent)
         part = sums_of_rows.finish()
         last_sent = part
         weight = part if weight is None else [a + b for a, b in zip(weight, part)]

time: 177 us -> 170 us (0.960)
  waiting for transfers between devices: 58.8 us -> 42.5 us
  Pallas kernels: 51.7 us -> 56.2 us
  other arithmetic: 9.59 us -> 12.9 us
  starting transfers between devices: 19.4 us -> 21.4 us
    ppermute x8, waiting for transfers between devices: 19.2 us -> 7.07 us  [exchange_bit(): lax.ppermute(value, 'dp', [(source, source ^ 1 << bit) for source in rang...]
    ppermute x9 -> x10, waiting for transfers between devices: 38.8 us -> 34.7 us  [passed_along(): return lax.ppermute(value, axis, pairs)]
    pallas_call x4, Pallas kernels: 5.33 us -> 8.72 us  [add_parts(): pl.pallas_call(functools.partial(add_kernel, count), grid=(heads,), in_sp...]
    add x8, other arithmetic: 5.81 us -> 8.43 us  [totals(): return [a + b.astype(jnp.float32) for a, b in zip(kept, got)]]
    slice x1 -> x0, local copies, waits for them, and re-layouts: 1.95 us -> none  [__init__(): columns = [og[:, :half], after(og[:, half:], hold)]]
    unnamed x64 -> x68, local copies, waits for them, and re-layouts: 6.76 us -> 8.29 us
    ppermute x9 -> x10, starting transfers between devices: 11.4 us -> 12.9 us  [passed_along(): return lax.ppermute(value, axis, pairs)]
    pallas_call x3 -> x4, Pallas kernels: 13.1 us -> 14.1 us  [forward(): pl.pallas_call(functools.partial(forward_kernel, count), grid=(heads,), i...]
  transfers between devices with their start and end apart: 18 -> 19, of which waited for: 9 -> 8; matrix products, arithmetic and copies ran while one was open for 11% -> 12% of each run, Pallas kernels for 22% -> 27%
where the time goes in v3:
time: 170 us; the launch traced here: 169 us
  Pallas kernels  56.2 us (33%)
  waiting for transfers between devices  42.5 us (25%)
  starting transfers between devices  21.4 us (13%)
  between operations  16.4 us (10%)
  local copies, waits for them, and re-layouts  15 us (9%)
  other arithmetic  12.9 us (8%)
  matrix products  5.09 us (3%)
    ppermute x10, waiting for transfers between devices, passed_along(): return lax.ppermute(value, axis, pairs)  34.7 us
    pallas_call x4, Pallas kernels, backward(): pl.pallas_call(functools.partial(backward_kernel, count), grid=(heads,),...  33.4 us
    pallas_call x4, Pallas kernels, forward(): pl.pallas_call(functools.partial(forward_kernel, count), grid=(heads,), i...  14.1 us
    ppermute x10, starting transfers between devices, passed_along(): return lax.ppermute(value, axis, pairs)  12.9 us
    pallas_call x4, Pallas kernels, add_parts(): pl.pallas_call(functools.partial(add_kernel, count), grid=(heads,), in_sp...  8.72 us
    ppermute x8, starting transfers between devices, exchange_bit(): lax.ppermute(value, 'dp', [(source, source ^ 1 << bit) for source in rang...  8.48 us
    add x8, other arithmetic, totals(): return [a + b.astype(jnp.float32) for a, b in zip(kept, got)]  8.43 us
    unnamed x68, local copies, waits for them, and re-layouts  8.29 us
  transfers between devices with their start and end apart: 19, of which 8 were waited for; matrix products, arithmetic and copies ran while one was open for 12% of the time, Pallas kernels for 27%

profile of v3, /device:TPU:0, one launch (start us, length us, event | category | flops | bytes accessed | tf_op | source)
XLA Modules:
  0.0 169.4 jit_solution(1966143805053392038)
XLA Ops:
  7.9 1.2 slice_bitcast_fusion
  9.1 0.9 pad_maximum_fusion
  10.0 3.0 %collective-permute-start.3 = (bf16[2,384,384]{2,1,0:T(8,128)(2,1)}, bf16[2,384,384]{2,1,0:T(8,128)(2,1)}, u32[]{:S(2)}, u32[]{:S(2)}) collective-permute-start(bf16[2,384,384]{2,1,0:T(8,128)(2,1)} %pad_maximum_fusion), channel_id=1, source_target_pairs={{0,1},{1,0},{2,3},{3,2},{4,5},{5,4},{6,7},{7,6},{8,9},{9,8},{10,11... | collective-permute-start | bytes 1769480 | tf_op jit(solution)/shard_map/ppermute | solution.py:31
  13.1 0.9 pad_maximum_fusion.1
  14.6 0.9 pad_maximum_fusion.2
  15.5 1.4 collective-permute-start.1
  17.0 0.9 pad_maximum_fusion.3
  21.1 6.4 %collective-permute-done.3.refs_0_ = bf16[2,384,384]{2,1,0:T(8,128)(2,1)} collective-permute-done((bf16[2,384,384]{2,1,0:T(8,128)(2,1)}, bf16[2,384,384]{2,1,0:T(8,128)(2,1)}, u32[]{:S(2)}, u32[]{:S(2)}) %collective-permute-start.3) | collective-permute-done | bytes 589856 | tf_op jit(solution)/shard_map/ppermute | solution.py:31
  27.5 3.5 %attend.4 = (bf16[1536,384]{1,0:T(8,128)(2,1)S(1)}, f32[3,8,384]{2,1,0:T(8,128)S(1)}) custom-call(f32[1]{0:T(128)} %bitcast.2.bias_ref, bf16[384,1536]{1,0:T(8,128)(2,1)S(1)} %bitcast.85, bf16[384,1536]{1,0:T(8,128)(2,1)S(1)} %bitcast.65, bf16[384,1536]{1,0:T(8,128)(2,1)S(1)} %bitcast.77, bf16[2,384,384]{2,1,0:T(8,128)(2,1)} %collective-permute-done.3.refs_0_), custom_call_target="tpu_custom_call" | custom-call | flops 452984832 | bytes 1769472 | tf_op jit(solution)/shard_map/attend/pallas_call | solution.py:124
  31.6 8.5 %collective-permute-done.2.refs_0_ = bf16[2,384,384]{2,1,0:T(8,128)(2,1)} collective-permute-done((bf16[2,384,384]{2,1,0:T(8,128)(2,1)}, bf16[2,384,384]{2,1,0:T(8,128)(2,1)}, u32[]{:S(2)}, u32[]{:S(2)}) %collective-permute-start.2) | collective-permute-done | bytes 589856 | tf_op jit(solution)/shard_map/ppermute | solution.py:31
  40.1 3.5 %attend.5 = (bf16[1536,384]{1,0:T(8,128)(2,1)S(1)}, f32[3,8,384]{2,1,0:T(8,128)S(1)}) custom-call(f32[1]{0:T(128)} %bitcast.2.bias_ref, bf16[384,1536]{1,0:T(8,128)(2,1)S(1)} %bitcast.86, bf16[384,1536]{1,0:T(8,128)(2,1)S(1)} %bitcast.66, bf16[384,1536]{1,0:T(8,128)(2,1)S(1)} %bitcast.78, ...), custom_call_target="tpu_custom_call", output_to_operand_aliasing={{0}: (5, {})} | custom-call | flops 452984832 | bytes 1769472 | tf_op jit(solution)/shard_map/attend/pallas_call | solution.py:124
  44.2 8.5 %collective-permute-done.1.refs_0_ = bf16[2,384,384]{2,1,0:T(8,128)(2,1)} collective-permute-done((bf16[2,384,384]{2,1,0:T(8,128)(2,1)}, bf16[2,384,384]{2,1,0:T(8,128)(2,1)}, u32[]{:S(2)}, u32[]{:S(2)}) %collective-permute-start.1) | collective-permute-done | bytes 589856 | tf_op jit(solution)/shard_map/ppermute | solution.py:31
  52.7 3.5 %attend.6 = (bf16[1536,384]{1,0:T(8,128)(2,1)S(1)}, f32[3,8,384]{2,1,0:T(8,128)S(1)}) custom-call(f32[1]{0:T(128)} %bitcast.2.bias_ref, bf16[384,1536]{1,0:T(8,128)(2,1)S(1)} %bitcast.87, bf16[384,1536]{1,0:T(8,128)(2,1)S(1)} %bitcast.67, bf16[384,1536]{1,0:T(8,128)(2,1)S(1)} %bitcast.79, ...), custom_call_target="tpu_custom_call", output_to_operand_aliasing={{0}: (5, {})} | custom-call | flops 452984832 | bytes 1769472 | tf_op jit(solution)/shard_map/attend/pallas_call | solution.py:124
  56.9 7.7 %collective-permute-done.refs_0_ = bf16[2,384,384]{2,1,0:T(8,128)(2,1)} collective-permute-done((bf16[2,384,384]{2,1,0:T(8,128)(2,1)}, bf16[2,384,384]{2,1,0:T(8,128)(2,1)}, u32[]{:S(2)}, u32[]{:S(2)}) %collective-permute-start) | collective-permute-done | bytes 589856 | tf_op jit(solution)/shard_map/ppermute | solution.py:31
  64.5 3.5 %attend.7 = (bf16[1536,384]{1,0:T(8,128)(2,1)S(1)}, f32[3,8,384]{2,1,0:T(8,128)S(1)}) custom-call(f32[1]{0:T(128)} %bitcast.2.bias_ref, bf16[384,1536]{1,0:T(8,128)(2,1)S(1)} %bitcast.88, bf16[384,1536]{1,0:T(8,128)(2,1)S(1)} %bitcast.68, bf16[384,1536]{1,0:T(8,128)(2,1)S(1)} %bitcast.80, ...), custom_call_target="tpu_custom_call", output_to_operand_aliasing={{0}: (5, {})} | custom-call | flops 452984832 | bytes 1769472 | tf_op jit(solution)/shard_map/attend/pallas_call | solution.py:124
  68.1 1.0 copy-done.3
  70.5 8.3 %attend_grad.4 = (bf16[384,1536]{1,0:T(8,128)(2,1)}, f32[2,384,384]{2,1,0:T(8,128)S(1)}, bf16[2,384,384]{2,1,0:T(8,128)(2,1)S(1)}) custom-call(f32[1]{0:T(128)} %bitcast.2.bias_ref, bf16[384,1536]{1,0:T(8,128)(2,1)S(1)} %bitcast.89, bf16[384,1536]{1,0:T(8,128)(2,1)S(1)} %bitcast.69, bf16[384,1536]{1,0:T(8,128)(2,1)S(1)} %bitcast.81, ...), custom_call_target="tpu_custom_call" | custom-call | flops 1000 | bytes 1000 | tf_op jit(solution)/shard_map/attend_grad/pallas_call | solution.py:151
  78.8 1.0 constant_dynamic-slice_fusion.1
  80.9 1.8 %multiply_convert_fusion = bf16[768,768]{1,0:T(8,128)(2,1)} fusion(bf16[768,384]{1,0:T(8,128)(2,1)S(1)} %bitcast.109, bf16[384,1536]{1,0:T(8,128)(2,1)S(1)} %bitcast.98), kind=kOutput, calls=%fused_computation.2 | convolution fusion | flops 454164480 | bytes 2359296 | tf_op jit(solution)/shard_map/dot_general | solution.py:25
  82.6 1.8 %multiply_convert_fusion.1 = bf16[768,768]{1,0:T(8,128)(2,1)} fusion(bf16[768,384]{1,0:T(8,128)(2,1)S(1)} %bitcast.110, bf16[384,1536]{1,0:T(8,128)(2,1)S(1)} %bitcast.99), kind=kOutput, calls=%fused_computation.3 | convolution fusion | flops 454164480 | bytes 2359296 | tf_op jit(solution)/shard_map/dot_general | solution.py:25
  84.9 1.8 %collective-permute-start.6 = (bf16[2,384,384]{2,1,0:T(8,128)(2,1)}, bf16[2,384,384]{2,1,0:T(8,128)(2,1)S(1)}, u32[]{:S(2)}, u32[]{:S(2)}) collective-permute-start(bf16[2,384,384]{2,1,0:T(8,128)(2,1)} %copy-done.21), channel_id=1, source_target_pairs={{0,1},{1,0},{2,3},{3,2},{4,5},{5,4},{6,7},{7,6},{8,9},{9,8},{10,11... | collective-permute-start | bytes 1769480 | tf_op jit(solution)/shard_map/ppermute | solution.py:31
  87.5 8.4 %attend_grad.5 = (bf16[384,1536]{1,0:T(8,128)(2,1)}, f32[2,384,384]{2,1,0:T(8,128)S(1)}, bf16[2,384,384]{2,1,0:T(8,128)(2,1)}) custom-call(f32[1]{0:T(128)} %bitcast.2.bias_ref, bf16[384,1536]{1,0:T(8,128)(2,1)S(1)} %bitcast.90, bf16[384,1536]{1,0:T(8,128)(2,1)S(1)} %bitcast.70, bf16[384,1536]{1,0:T(8,128)(2,1)S(1)} %bitcast.82, ...), custom_call_target="tpu_custom_call", output_to_operand_aliasing={{0}: (9, {})} | custom-call | flops 1000 | bytes 1000 | tf_op jit(solution)/shard_map/attend_grad/pallas_call | solution.py:151
  97.7 3.7 %collective-permute-done.6.refs_0_ = bf16[2,384,384]{2,1,0:T(8,128)(2,1)S(1)} collective-permute-done((bf16[2,384,384]{2,1,0:T(8,128)(2,1)}, bf16[2,384,384]{2,1,0:T(8,128)(2,1)S(1)}, u32[]{:S(2)}, u32[]{:S(2)}) %collective-permute-start.6) | collective-permute-done | bytes 589856 | tf_op jit(solution)/shard_map/ppermute | solution.py:31
  101.4 1.8 %copy_add_fusion = f32[2,2,2,96,768]{4,3,2,0,1:T(8,128)S(1)} fusion(f32[2,2,2,96,768]{4,3,2,1,0:T(8,128)S(1)} %bitcast.106, bf16[2,2,2,96,768]{4,3,2,1,0:T(8,128)(2,1)} %bitcast.20), kind=kLoop, calls=%fused_computation | loop fusion | flops 1179648 | bytes 5898240 | tf_op jit(solution)/shard_map/add | solution.py:238
  103.2 1.0 fusion.1
  104.2 1.8 %collective-permute-start.8 = (bf16[2,2,96,768]{3,2,1,0:T(8,128)(2,1)}, bf16[2,2,96,768]{3,2,1,0:T(8,128)(2,1)}, u32[]{:S(2)}, u32[]{:S(2)}) collective-permute-start(bf16[2,2,96,768]{3,2,1,0:T(8,128)(2,1)} %fusion.1), channel_id=1, source_target_pairs={{0,8},{2,10},{4,12},{6,14},{8,0},{10,2},{12,4},{14,6},{16,24},{18,... | collective-permute-start | bytes 1769480 | tf_op jit(solution)/shard_map/ppermute | solution.py:194
  106.0 1.6 copy_add_fusion.1
  107.6 1.0 fusion
  109.2 1.5 collective-permute-start.7
  111.5 8.4 %attend_grad.6 = (bf16[384,1536]{1,0:T(8,128)(2,1)}, f32[2,384,384]{2,1,0:T(8,128)S(1)}, bf16[2,384,384]{2,1,0:T(8,128)(2,1)}) custom-call(f32[1]{0:T(128)} %bitcast.2.bias_ref, bf16[384,1536]{1,0:T(8,128)(2,1)S(1)} %bitcast.91, bf16[384,1536]{1,0:T(8,128)(2,1)S(1)} %bitcast.71, bf16[384,1536]{1,0:T(8,128)(2,1)S(1)} %bitcast.83, ...), custom_call_target="tpu_custom_call", output_to_operand_aliasing={{0}: (9, {})} | custom-call | flops 1000 | bytes 1000 | tf_op jit(solution)/shard_map/attend_grad/pallas_call | solution.py:151
  119.9 1.6 collective-permute-start.12
  121.5 1.2 collective-permute-done.7
  122.7 1.2 bitcast_add_fusion
  123.9 1.6 bitcast_add_fusion.1
  127.1 2.6 %collective-permute-start.11 = (bf16[2,96,768]{2,1,0:T(8,128)(2,1)}, bf16[2,96,768]{2,1,0:T(8,128)(2,1)}, u32[]{:S(2)}, u32[]{:S(2)}) collective-permute-start(bf16[2,96,768]{2,1,0:T(8,128)(2,1)} %fusion.7), channel_id=1, source_target_pairs={{0,16},{2,18},{4,20},{6,22},{8,24},{10,26},{12,28},{14,30},{16,0},... | collective-permute-start | bytes 884744 | tf_op jit(solution)/shard_map/ppermute | solution.py:194
  130.9 8.3 %attend_grad.7 = (bf16[384,1536]{1,0:T(8,128)(2,1)}, f32[2,384,384]{2,1,0:T(8,128)S(1)}, bf16[2,384,384]{2,1,0:T(8,128)(2,1)S(1)}) custom-call(f32[1]{0:T(128)} %bitcast.2.bias_ref, bf16[384,1536]{1,0:T(8,128)(2,1)S(1)} %bitcast.92, bf16[384,1536]{1,0:T(8,128)(2,1)S(1)} %bitcast.72, bf16[384,1536]{1,0:T(8,128)(2,1)S(1)} %bitcast.84, ...), custom_call_target="tpu_custom_call", output_to_operand_aliasing={{0}: (9, {})} | custom-call | flops 1000 | bytes 1000 | tf_op jit(solution)/shard_map/attend_grad/pallas_call | solution.py:151
  139.2 1.5 collective-permute-start.15
  140.8 1.1 collective-permute-done.10
  141.9 1.0 bitcast_add_fusion.3
  143.1 1.1 bitcast_add_fusion.2
  144.2 1.6 collective-permute-start.14
  145.8 4.8 %collective-permute-done.13 = bf16[96,768]{1,0:T(8,128)(2,1)S(1)} collective-permute-done((bf16[96,768]{1,0:T(8,128)(2,1)S(1)}, bf16[96,768]{1,0:T(8,128)(2,1)S(1)}, u32[]{:S(2)}, u32[]{:S(2)}) %collective-permute-start.13) | collective-permute-done | bytes 147488 | tf_op jit(solution)/shard_map/ppermute | solution.py:194
  150.6 1.5 collective-permute-start.16
  152.8 1.5 add_parts.4
  154.4 2.9 %add_parts.5 = (bf16[384,1536]{1,0:T(8,128)(2,1)}, bf16[384,1536]{1,0:T(8,128)(2,1)}) custom-call(f32[2,384,384]{2,1,0:T(8,128)S(1)} %copy-done.8, bf16[2,384,384]{2,1,0:T(8,128)(2,1)} %collective-permute-done.9.refs_0_, bf16[384,1536]{1,0:T(8,128)(2,1)} %get-tuple-element.92.refs_1_, ...), custom_call_target="tpu_custom_call", output_to_operand_aliasing={{0}: (2, {}), {1}: (3, {})} | custom-call | bytes 2359296 | tf_op jit(solution)/shard_map/add_parts/pallas_call | solution.py:179
  157.2 2.8 %add_parts.6 = (bf16[384,1536]{1,0:T(8,128)(2,1)}, bf16[384,1536]{1,0:T(8,128)(2,1)}) custom-call(f32[2,384,384]{2,1,0:T(8,128)S(1)} %copy-done.10, bf16[2,384,384]{2,1,0:T(8,128)(2,1)} %collective-permute-done.12.refs_0_, bf16[384,1536]{1,0:T(8,128)(2,1)} %get-tuple-element.94.refs_1_, ...), custom_call_target="tpu_custom_call", output_to_operand_aliasing={{0}: (2, {}), {1}: (3, {})} | custom-call | bytes 2359296 | tf_op jit(solution)/shard_map/add_parts/pallas_call | solution.py:179
  160.1 0.9 pad_maximum_fusion.4
  161.0 1.5 add_parts.7
  (106 shorter events, 15.3 us)
Async XLA Ops:
  7.2 62.5 %all-gather.2.cloned.1.call-start = ((), (), s32[]{:S(2)}) async-start(), calls=%async_computation | async-start | bytes 5013504 | tf_op jit(solution)/shard_map/all_gather | solution.py:269
  7.9 5.1 %copy-start.1 = (bf16[1,384,1536]{2,1,0:T(8,128)(2,1)S(1)}, bf16[1,384,1536]{2,1,0:T(8,128)(2,1)}, u32[]{:S(2)}) copy-start(bf16[1,384,1536]{2,1,0:T(8,128)(2,1)} %param.9) | copy-start | bytes 3538948
  9.1 3.9 %copy-start = (bf16[1,384,1536]{2,1,0:T(8,128)(2,1)S(1)}, bf16[1,384,1536]{2,1,0:T(8,128)(2,1)}, u32[]{:S(2)}) copy-start(bf16[1,384,1536]{2,1,0:T(8,128)(2,1)} %param.8) | copy-start | bytes 3538948
  10.0 17.4 %collective-permute-start.3 = (bf16[2,384,384]{2,1,0:T(8,128)(2,1)}, bf16[2,384,384]{2,1,0:T(8,128)(2,1)}, u32[]{:S(2)}, u32[]{:S(2)}) collective-permute-start(bf16[2,384,384]{2,1,0:T(8,128)(2,1)} %pad_maximum_fusion), channel_id=1, source_target_pairs={{0,1},{1,0},{2,3},{3,2},{4,5},{5,4},{6,7},{7,6},{8,9},{9,8},{10,11... | collective-permute-start | bytes 1769480 | tf_op jit(solution)/shard_map/ppermute | solution.py:31
  14.0 26.1 %collective-permute-start.2 = (bf16[2,384,384]{2,1,0:T(8,128)(2,1)}, bf16[2,384,384]{2,1,0:T(8,128)(2,1)}, u32[]{:S(2)}, u32[]{:S(2)}) collective-permute-start(bf16[2,384,384]{2,1,0:T(8,128)(2,1)} %pad_maximum_fusion.1), channel_id=1, source_target_pairs={{0,1},{1,0},{2,3},{3,2},{4,5},{5,4},{6,7},{7,6},{8,9},{9,8},{10,11... | collective-permute-start | bytes 1769480 | tf_op jit(solution)/shard_map/ppermute | solution.py:31
  15.5 3.7 %copy-start.33 = (s32[2,3]{1,0:T(2,128)S(1)}, s32[2,3]{1,0:T(2,128)}, u32[]{:S(2)}) copy-start(s32[2,3]{1,0:T(2,128)} %param.13) | copy-start | bytes 76
  15.5 11.9 %copy-start.2 = (bf16[1,384,1536]{2,1,0:T(8,128)(2,1)S(1)}, bf16[1,384,1536]{2,1,0:T(8,128)(2,1)}, u32[]{:S(2)}) copy-start(bf16[1,384,1536]{2,1,0:T(8,128)(2,1)} %param.7) | copy-start | bytes 3538948
  15.5 37.2 %collective-permute-start.1 = (bf16[2,384,384]{2,1,0:T(8,128)(2,1)}, bf16[2,384,384]{2,1,0:T(8,128)(2,1)}, u32[]{:S(2)}, u32[]{:S(2)}) collective-permute-start(bf16[2,384,384]{2,1,0:T(8,128)(2,1)} %pad_maximum_fusion.2), channel_id=1, source_target_pairs={{0,1},{1,0},{2,3},{3,2},{4,5},{5,4},{6,7},{7,6},{8,9},{9,8},{10,11... | collective-permute-start | bytes 1769480 | tf_op jit(solution)/shard_map/ppermute | solution.py:31
  17.9 46.6 %collective-permute-start = (bf16[2,384,384]{2,1,0:T(8,128)(2,1)}, bf16[2,384,384]{2,1,0:T(8,128)(2,1)}, u32[]{:S(2)}, u32[]{:S(2)}) collective-permute-start(bf16[2,384,384]{2,1,0:T(8,128)(2,1)} %pad_maximum_fusion.3), channel_id=1, source_target_pairs={{0,1},{1,0},{2,3},{3,2},{4,5},{5,4},{6,7},{7,6},{8,9},{9,8},{10,11... | collective-permute-start | bytes 1769480 | tf_op jit(solution)/shard_map/ppermute | solution.py:31
  68.1 1.0 copy-start.3
  69.7 0.8 copy-start.20
  70.5 8.3 %copy-start.4 = (bf16[1536,384]{1,0:T(8,128)(2,1)S(1)}, bf16[1536,384]{1,0:T(8,128)(2,1)}, u32[]{:S(2)}) copy-start(bf16[1536,384]{1,0:T(8,128)(2,1)} %copy-done.3) | copy-start | bytes 3538948
  78.7 1.2 copy-start.5
  78.7 1.4 copy-start.21
  78.8 2.1 %copy-start.22 = (bf16[1,384,1536]{2,1,0:T(8,128)(2,1)S(1)}, bf16[1,384,1536]{2,1,0:T(8,128)(2,1)}, u32[]{:S(2)}) copy-start(bf16[1,384,1536]{2,1,0:T(8,128)(2,1)} %param.10) | copy-start | bytes 3538948
  84.4 16.9 %collective-permute-start.4 = (bf16[768,768]{1,0:T(8,128)(2,1)}, bf16[768,768]{1,0:T(8,128)(2,1)}, u32[]{:S(2)}, u32[]{:S(2)}) collective-permute-start(bf16[768,768]{1,0:T(8,128)(2,1)} %multiply_convert_fusion.1), channel_id=1, source_target_pairs={{0,2},{2,0},{4,6},{6,4},{8,10},{10,8},{12,14},{14,12},{16,18},{18,... | collective-permute-start | bytes 3538952 | tf_op jit(solution)/shard_map/ppermute | solution.py:194
  84.4 16.9 %collective-permute-start.5 = (bf16[768,768]{1,0:T(8,128)(2,1)}, bf16[768,768]{1,0:T(8,128)(2,1)}, u32[]{:S(2)}, u32[]{:S(2)}) collective-permute-start(bf16[768,768]{1,0:T(8,128)(2,1)} %multiply_convert_fusion), channel_id=1, source_target_pairs={{0,2},{2,0},{4,6},{6,4},{8,10},{10,8},{12,14},{14,12},{16,18},{18,... | collective-permute-start | bytes 3538952 | tf_op jit(solution)/shard_map/ppermute | solution.py:194
  84.9 16.4 %collective-permute-start.6 = (bf16[2,384,384]{2,1,0:T(8,128)(2,1)}, bf16[2,384,384]{2,1,0:T(8,128)(2,1)S(1)}, u32[]{:S(2)}, u32[]{:S(2)}) collective-permute-start(bf16[2,384,384]{2,1,0:T(8,128)(2,1)} %copy-done.21), channel_id=1, source_target_pairs={{0,1},{1,0},{2,3},{3,2},{4,5},{5,4},{6,7},{7,6},{8,9},{9,8},{10,11... | collective-permute-start | bytes 1769480 | tf_op jit(solution)/shard_map/ppermute | solution.py:31
  86.7 0.8 copy-start.18
  87.5 8.6 %copy-start.23 = (bf16[1,384,1536]{2,1,0:T(8,128)(2,1)S(1)}, bf16[1,384,1536]{2,1,0:T(8,128)(2,1)}, u32[]{:S(2)}) copy-start(bf16[1,384,1536]{2,1,0:T(8,128)(2,1)} %param.10) | copy-start | bytes 3538948
  87.5 8.6 %copy-start.28 = (bf16[8,1,96,384]{3,2,1,0:T(8,128)(2,1)S(1)}, bf16[8,1,96,384]{3,2,1,0:T(8,128)(2,1)}, u32[]{:S(2)}) copy-start(bf16[8,1,96,384]{3,2,1,0:T(8,128)(2,1)} %get-tuple-element.111) | copy-start | bytes 1769476
  95.8 1.0 copy-start.7
  95.8 25.7 %collective-permute-start.9 = (bf16[2,384,384]{2,1,0:T(8,128)(2,1)}, bf16[2,384,384]{2,1,0:T(8,128)(2,1)}, u32[]{:S(2)}, u32[]{:S(2)}) collective-permute-start(bf16[2,384,384]{2,1,0:T(8,128)(2,1)} %get-tuple-element.68), channel_id=1, source_target_pairs={{0,1},{1,0},{2,3},{3,2},{4,5},{5,4},{6,7},{7,6},{8,9},{9,8},{10,11... | collective-permute-start | bytes 1769480 | tf_op jit(solution)/shard_map/ppermute | solution.py:31
  101.3 1.8 %copy-start.11 = (bf16[2,384,384]{2,1,0:T(8,128)(2,1)}, bf16[2,384,384]{2,1,0:T(8,128)(2,1)S(1)}, u32[]{:S(2)}) copy-start(bf16[2,384,384]{2,1,0:T(8,128)(2,1)S(1)} %collective-permute-done.6.refs_0_) | copy-start | bytes 1769476
  103.2 4.4 %copy-start.24 = (f32[2,2,2,96,768]{4,3,2,0,1:T(8,128)}, f32[2,2,2,96,768]{4,3,2,0,1:T(8,128)S(1)}, u32[]{:S(2)}) copy-start(f32[2,2,2,96,768]{4,3,2,0,1:T(8,128)S(1)} %copy_add_fusion) | copy-start | bytes 7077892
  104.2 17.3 %collective-permute-start.8 = (bf16[2,2,96,768]{3,2,1,0:T(8,128)(2,1)}, bf16[2,2,96,768]{3,2,1,0:T(8,128)(2,1)}, u32[]{:S(2)}, u32[]{:S(2)}) collective-permute-start(bf16[2,2,96,768]{3,2,1,0:T(8,128)(2,1)} %fusion.1), channel_id=1, source_target_pairs={{0,8},{2,10},{4,12},{6,14},{8,0},{10,2},{12,4},{14,6},{16,24},{18,... | collective-permute-start | bytes 1769480 | tf_op jit(solution)/shard_map/ppermute | solution.py:194
  107.6 1.6 copy-start.26
  109.2 13.5 %collective-permute-start.7 = (bf16[2,2,96,768]{3,2,0,1:T(8,128)(2,1)}, bf16[2,2,96,768]{3,2,0,1:T(8,128)(2,1)}, u32[]{:S(2)}, u32[]{:S(2)}) collective-permute-start(bf16[2,2,96,768]{3,2,0,1:T(8,128)(2,1)} %fusion), channel_id=1, source_target_pairs={{0,4},{2,6},{4,0},{6,2},{8,12},{10,14},{12,8},{14,10},{16,20},{18,... | collective-permute-start | bytes 1769480 | tf_op jit(solution)/shard_map/ppermute | solution.py:194
  110.7 0.8 copy-start.16
  111.5 11.2 %copy-start.25 = (f32[2,2,2,96,768]{4,3,2,0,1:T(8,128)S(1)}, f32[2,2,2,96,768]{4,3,2,0,1:T(8,128)}, u32[]{:S(2)}) copy-start(f32[2,2,2,96,768]{4,3,2,0,1:T(8,128)} %copy-done.24) | copy-start | bytes 7077892
  119.9 4.0 %copy-start.9 = (f32[2,384,384]{2,1,0:T(8,128)}, f32[2,384,384]{2,1,0:T(8,128)S(1)}, u32[]{:S(2)}) copy-start(f32[2,384,384]{2,1,0:T(8,128)S(1)} %get-tuple-element.87.own_ref) | copy-start | bytes 3538948
  119.9 4.0 %copy-start.27 = (f32[2,2,2,96,768]{4,3,0,1,2:T(8,128)S(1)}, f32[2,2,2,96,768]{4,3,0,1,2:T(8,128)}, u32[]{:S(2)}) copy-start(f32[2,2,2,96,768]{4,3,0,1,2:T(8,128)} %copy-done.26) | copy-start | bytes 7077892
  119.9 20.8 %collective-permute-start.12 = (bf16[2,384,384]{2,1,0:T(8,128)(2,1)}, bf16[2,384,384]{2,1,0:T(8,128)(2,1)}, u32[]{:S(2)}, u32[]{:S(2)}) collective-permute-start(bf16[2,384,384]{2,1,0:T(8,128)(2,1)} %get-tuple-element.74), channel_id=1, source_target_pairs={{0,1},{1,0},{2,3},{3,2},{4,5},{5,4},{6,7},{7,6},{8,9},{9,8},{10,11... | collective-permute-start | bytes 1769480 | tf_op jit(solution)/shard_map/ppermute | solution.py:31
  123.9 2.5 %copy-start.29 = (f32[2,2,96,768]{3,2,1,0:T(8,128)}, f32[2,2,96,768]{3,2,1,0:T(8,128)S(1)}, u32[]{:S(2)}) copy-start(f32[2,2,96,768]{3,2,1,0:T(8,128)S(1)} %bitcast_add_fusion) | copy-start | bytes 3538948
  125.5 1.6 copy-start.31
  127.1 13.6 %collective-permute-start.11 = (bf16[2,96,768]{2,1,0:T(8,128)(2,1)}, bf16[2,96,768]{2,1,0:T(8,128)(2,1)}, u32[]{:S(2)}, u32[]{:S(2)}) collective-permute-start(bf16[2,96,768]{2,1,0:T(8,128)(2,1)} %fusion.7), channel_id=1, source_target_pairs={{0,16},{2,18},{4,20},{6,22},{8,24},{10,26},{12,28},{14,30},{16,0},... | collective-permute-start | bytes 884744 | tf_op jit(solution)/shard_map/ppermute | solution.py:194
  129.7 12.2 %collective-permute-start.10 = (bf16[2,96,768]{2,1,0:T(8,128)(2,1)}, bf16[2,96,768]{2,1,0:T(8,128)(2,1)}, u32[]{:S(2)}, u32[]{:S(2)}) collective-permute-start(bf16[2,96,768]{2,1,0:T(8,128)(2,1)} %fusion.6), channel_id=1, source_target_pairs={{0,8},{2,10},{4,12},{6,14},{8,0},{10,2},{12,4},{14,6},{16,24},{18,... | collective-permute-start | bytes 884744 | tf_op jit(solution)/shard_map/ppermute | solution.py:194
  130.9 11.0 %copy-start.32 = (f32[2,2,96,768]{3,2,0,1:T(8,128)S(1)}, f32[2,2,96,768]{3,2,0,1:T(8,128)}, u32[]{:S(2)}) copy-start(f32[2,2,96,768]{3,2,0,1:T(8,128)} %copy-done.31) | copy-start | bytes 3538948
  139.2 3.8 %copy-start.30 = (f32[2,2,96,768]{3,2,1,0:T(8,128)S(1)}, f32[2,2,96,768]{3,2,1,0:T(8,128)}, u32[]{:S(2)}) copy-start(f32[2,2,96,768]{3,2,1,0:T(8,128)} %copy-done.29) | copy-start | bytes 3538948
  139.2 21.7 %collective-permute-start.15 = (bf16[2,384,384]{2,1,0:T(8,128)(2,1)S(1)}, bf16[2,384,384]{2,1,0:T(8,128)(2,1)S(1)}, u32[]{:S(2)}, u32[]{:S(2)}) collective-permute-start(bf16[2,384,384]{2,1,0:T(8,128)(2,1)S(1)} %get-tuple-element.82), channel_id=1, source_target_pairs={{0,1},{1,0},{2,3},{3,2},{4,5},{5,4},{6,7},{7,6},{8,9},{9,8},{10,11... | collective-permute-start | bytes 1769480 | tf_op jit(solution)/shard_map/ppermute | solution.py:31
  143.0 9.9 %copy-start.6 = (f32[2,384,384]{2,1,0:T(8,128)S(1)}, f32[2,384,384]{2,1,0:T(8,128)}, u32[]{:S(2)}) copy-start(f32[2,384,384]{2,1,0:T(8,128)} %copy-done.5) | copy-start | bytes 3538948
  143.0 9.9 %copy-start.12 = (bf16[2,384,384]{2,1,0:T(8,128)(2,1)S(1)}, bf16[2,384,384]{2,1,0:T(8,128)(2,1)}, u32[]{:S(2)}) copy-start(bf16[2,384,384]{2,1,0:T(8,128)(2,1)} %copy-done.11) | copy-start | bytes 1769476
  143.0 7.6 %collective-permute-start.13 = (bf16[96,768]{1,0:T(8,128)(2,1)S(1)}, bf16[96,768]{1,0:T(8,128)(2,1)S(1)}, u32[]{:S(2)}, u32[]{:S(2)}) collective-permute-start(bf16[96,768]{1,0:T(8,128)(2,1)S(1)} %fusion.8), channel_id=1, source_target_pairs={{0,16},{2,18},{4,20},{6,22},{8,24},{10,26},{12,28},{14,30},{16,0},... | collective-permute-start | bytes 442376 | tf_op jit(solution)/shard_map/ppermute | solution.py:194
  144.2 7.9 %collective-permute-start.14 = (bf16[96,768]{1,0:T(8,128)(2,1)S(1)}, bf16[96,768]{1,0:T(8,128)(2,1)S(1)}, u32[]{:S(2)}, u32[]{:S(2)}) collective-permute-start(bf16[96,768]{1,0:T(8,128)(2,1)S(1)} %fusion.9), channel_id=1, source_target_pairs={{0,4},{2,6},{4,0},{6,2},{8,12},{10,14},{12,8},{14,10},{16,20},{18,... | collective-permute-start | bytes 442376 | tf_op jit(solution)/shard_map/ppermute | solution.py:194
  150.6 3.8 %copy-start.8 = (f32[2,384,384]{2,1,0:T(8,128)S(1)}, f32[2,384,384]{2,1,0:T(8,128)}, u32[]{:S(2)}) copy-start(f32[2,384,384]{2,1,0:T(8,128)} %copy-done.7) | copy-start | bytes 3538948
  150.6 9.4 %collective-permute-start.16 = (bf16[96,768]{1,0:T(8,128)(2,1)S(1)}, bf16[96,768]{1,0:T(8,128)(2,1)S(1)}, u32[]{:S(2)}, u32[]{:S(2)}) collective-permute-start(bf16[96,768]{1,0:T(8,128)(2,1)S(1)} %bitcast_add_fusion.5), channel_id=1, source_target_pairs={{0,1},{1,0},{2,3},{3,2},{4,5},{5,4},{6,7},{7,6},{8,9},{9,8},{10,11... | collective-permute-start | bytes 442376 | tf_op jit(solution)/shard_map/ppermute | solution.py:31
  152.2 7.9 %collective-permute-start.17 = (bf16[96,768]{1,0:T(8,128)(2,1)S(1)}, bf16[96,768]{1,0:T(8,128)(2,1)S(1)}, u32[]{:S(2)}, u32[]{:S(2)}) collective-permute-start(bf16[96,768]{1,0:T(8,128)(2,1)S(1)} %bitcast_add_fusion.4), channel_id=1, source_target_pairs={{0,1},{1,0},{2,3},{3,2},{4,5},{5,4},{6,7},{7,6},{8,9},{9,8},{10,11... | collective-permute-start | bytes 442376 | tf_op jit(solution)/shard_map/ppermute | solution.py:31
  154.4 2.9 %copy-start.10 = (f32[2,384,384]{2,1,0:T(8,128)S(1)}, f32[2,384,384]{2,1,0:T(8,128)}, u32[]{:S(2)}) copy-start(f32[2,384,384]{2,1,0:T(8,128)} %copy-done.9) | copy-start | bytes 3538948
  (5 other events, 3.2 us)
Sparse Core Ops, SparseCore 0:
  10.3 56.0 all-gather.1

commit v4 on v3

--- a/solution.py
+++ b/solution.py
@@ -10,8 +10,8 @@
 
 HEADS = 12
 HS = 128
-CHUNKS = (3, 3, 3, 3)
-GRAD_CHUNKS = ((0, 0, 3), (1, 0, 3), (2, 0, 3), (3, 0, 3))
+CHUNKS = (3, 4, 3, 2)
+GRAD_CHUNKS = ((0, 0, 3), (1, 0, 4), (2, 0, 3), (3, 0, 2))
 SCALE = HS ** (-0.5)
 LOG2E = 1.4426950408889634
 VMEM_LIMIT = 48 * 1024 * 1024
@@ -306,11 +306,12 @@
             else:
                 sums_of_rows.step((away, pending[turn - 1][2]))
             bias = after(bias, sums_of_rows.sent)
+        early_sent = sums_of_rows.sent
         part = sums_of_rows.finish()
         last_sent = part
         weight = part if weight is None else [a + b for a, b in zip(weight, part)]
-        for span, own, received in pending:
-            own = after(own, last_sent)
+        for turn, (span, own, received) in enumerate(pending):
+            own = after(own, early_sent if turn < 2 else last_sent)
             sums = add_parts(*span, tile_len, width, own, received, sums)
         outs.append((dq, *sums))
     if seq_count == 2:

time: 170 us -> 167 us (0.982)
  waiting for transfers between devices: 42.5 us -> 39.2 us
    ppermute x8, waiting for transfers between devices: 7.07 us -> 5.22 us  [exchange_bit(): lax.ppermute(value, 'dp', [(source, source ^ 1 << bit) for source in rang...]
    unnamed x68 -> x66, local copies, waits for them, and re-layouts: 8.29 us -> 7.7 us
  transfers between devices with their start and end apart: 19 -> 19, of which waited for: 8 -> 9; matrix products, arithmetic and copies ran while one was open for 12% -> 12% of each run, Pallas kernels for 27% -> 29%
where the time goes in v4:
time: 167 us; the launch traced here: 166 us
  Pallas kernels  55.8 us (33%)
  waiting for transfers between devices  39.2 us (23%)
  starting transfers between devices  22 us (13%)
  between operations  16.3 us (10%)
  local copies, waits for them, and re-layouts  14.4 us (9%)
  other arithmetic  12.9 us (8%)
  matrix products  5.09 us (3%)
    ppermute x10, waiting for transfers between devices, passed_along(): return lax.ppermute(value, axis, pairs)  33.3 us
    pallas_call x4, Pallas kernels, backward(): pl.pallas_call(functools.partial(backward_kernel, count), grid=(heads,),...  33.2 us
    pallas_call x4, Pallas kernels, forward(): pl.pallas_call(functools.partial(forward_kernel, count), grid=(heads,), i...  14 us
    ppermute x10, starting transfers between devices, passed_along(): return lax.ppermute(value, axis, pairs)  13.6 us
    pallas_call x4, Pallas kernels, add_parts(): pl.pallas_call(functools.partial(add_kernel, count), grid=(heads,), in_sp...  8.6 us
    add x8, other arithmetic, totals(): return [a + b.astype(jnp.float32) for a, b in zip(kept, got)]  8.42 us
    ppermute x8, starting transfers between devices, exchange_bit(): lax.ppermute(value, 'dp', [(source, source ^ 1 << bit) for source in rang...  8.31 us
    unnamed x66, local copies, waits for them, and re-layouts  7.7 us
  transfers between devices with their start and end apart: 19, of which 9 were waited for; matrix products, arithmetic and copies ran while one was open for 12% of the time, Pallas kernels for 29%

profile of v4, /device:TPU:0, one launch (start us, length us, event | category | flops | bytes accessed | tf_op | source)
XLA Modules:
  0.0 165.6 jit_solution(8570737218705007559)
XLA Ops:
  7.9 1.2 slice_bitcast_fusion.2
  9.1 0.9 pad_maximum_fusion.1
  10.0 3.0 %collective-permute-start.3 = (bf16[2,384,384]{2,1,0:T(8,128)(2,1)}, bf16[2,384,384]{2,1,0:T(8,128)(2,1)}, u32[]{:S(2)}, u32[]{:S(2)}) collective-permute-start(bf16[2,384,384]{2,1,0:T(8,128)(2,1)} %pad_maximum_fusion.1), channel_id=1, source_target_pairs={{0,1},{1,0},{2,3},{3,2},{4,5},{5,4},{6,7},{7,6},{8,9},{9,8},{10,11... | collective-permute-start | bytes 1769480 | tf_op jit(solution)/shard_map/ppermute | solution.py:31
  13.1 0.9 pad_maximum_fusion
  14.7 0.9 pad_maximum_fusion.2
  15.6 1.4 collective-permute-start.1
  20.9 6.5 %collective-permute-done.3.refs_0_ = bf16[2,384,384]{2,1,0:T(8,128)(2,1)} collective-permute-done((bf16[2,384,384]{2,1,0:T(8,128)(2,1)}, bf16[2,384,384]{2,1,0:T(8,128)(2,1)}, u32[]{:S(2)}, u32[]{:S(2)}) %collective-permute-start.3) | collective-permute-done | bytes 589856 | tf_op jit(solution)/shard_map/ppermute | solution.py:31
  27.5 3.5 %attend.4 = (bf16[1536,384]{1,0:T(8,128)(2,1)S(1)}, f32[3,8,384]{2,1,0:T(8,128)S(1)}) custom-call(f32[1]{0:T(128)} %bitcast.2.bias_ref, bf16[384,1536]{1,0:T(8,128)(2,1)S(1)} %bitcast.85, bf16[384,1536]{1,0:T(8,128)(2,1)S(1)} %bitcast.65, bf16[384,1536]{1,0:T(8,128)(2,1)S(1)} %bitcast.77, bf16[2,384,384]{2,1,0:T(8,128)(2,1)} %collective-permute-done.3.refs_0_), custom_call_target="tpu_custom_call" | custom-call | flops 452984832 | bytes 1769472 | tf_op jit(solution)/shard_map/attend/pallas_call | solution.py:124
  31.6 12.7 %collective-permute-done.2.refs_0_ = bf16[2,384,512]{2,1,0:T(8,128)(2,1)} collective-permute-done((bf16[2,384,512]{2,1,0:T(8,128)(2,1)}, bf16[2,384,512]{2,1,0:T(8,128)(2,1)}, u32[]{:S(2)}, u32[]{:S(2)}) %collective-permute-start.2) | collective-permute-done | bytes 786464 | tf_op jit(solution)/shard_map/ppermute | solution.py:31
  44.3 4.4 %attend.5 = (bf16[1536,384]{1,0:T(8,128)(2,1)S(1)}, f32[4,8,384]{2,1,0:T(8,128)S(1)}) custom-call(f32[1]{0:T(128)} %bitcast.2.bias_ref, bf16[384,1536]{1,0:T(8,128)(2,1)S(1)} %bitcast.86, bf16[384,1536]{1,0:T(8,128)(2,1)S(1)} %bitcast.66, bf16[384,1536]{1,0:T(8,128)(2,1)S(1)} %bitcast.78, ...), custom_call_target="tpu_custom_call", output_to_operand_aliasing={{0}: (5, {})} | custom-call | flops 603979776 | bytes 2359296 | tf_op jit(solution)/shard_map/attend/pallas_call | solution.py:124
  48.7 8.2 %collective-permute-done.1.refs_0_ = bf16[2,384,384]{2,1,0:T(8,128)(2,1)} collective-permute-done((bf16[2,384,384]{2,1,0:T(8,128)(2,1)}, bf16[2,384,384]{2,1,0:T(8,128)(2,1)}, u32[]{:S(2)}, u32[]{:S(2)}) %collective-permute-start.1) | collective-permute-done | bytes 589856 | tf_op jit(solution)/shard_map/ppermute | solution.py:31
  56.9 3.5 %attend.6 = (bf16[1536,384]{1,0:T(8,128)(2,1)S(1)}, f32[3,8,384]{2,1,0:T(8,128)S(1)}) custom-call(f32[1]{0:T(128)} %bitcast.2.bias_ref, bf16[384,1536]{1,0:T(8,128)(2,1)S(1)} %bitcast.87, bf16[384,1536]{1,0:T(8,128)(2,1)S(1)} %bitcast.67, bf16[384,1536]{1,0:T(8,128)(2,1)S(1)} %bitcast.79, ...), custom_call_target="tpu_custom_call", output_to_operand_aliasing={{0}: (5, {})} | custom-call | flops 452984832 | bytes 1769472 | tf_op jit(solution)/shard_map/attend/pallas_call | solution.py:124
  61.1 3.5 %collective-permute-done.refs_0_ = bf16[2,384,256]{2,1,0:T(8,128)(2,1)} collective-permute-done((bf16[2,384,256]{2,1,0:T(8,128)(2,1)}, bf16[2,384,256]{2,1,0:T(8,128)(2,1)}, u32[]{:S(2)}, u32[]{:S(2)}) %collective-permute-start) | collective-permute-done | bytes 393248 | tf_op jit(solution)/shard_map/ppermute | solution.py:31
  64.5 2.5 %attend.7 = (bf16[1536,384]{1,0:T(8,128)(2,1)S(1)}, f32[2,8,384]{2,1,0:T(8,128)S(1)}) custom-call(f32[1]{0:T(128)} %bitcast.2.bias_ref, bf16[384,1536]{1,0:T(8,128)(2,1)S(1)} %bitcast.88, bf16[384,1536]{1,0:T(8,128)(2,1)S(1)} %bitcast.68, bf16[384,1536]{1,0:T(8,128)(2,1)S(1)} %bitcast.80, ...), custom_call_target="tpu_custom_call", output_to_operand_aliasing={{0}: (5, {})} | custom-call | flops 301989888 | bytes 1179648 | tf_op jit(solution)/shard_map/attend/pallas_call | solution.py:124
  67.1 1.0 copy-done.3
  69.5 8.3 %attend_grad.4 = (bf16[384,1536]{1,0:T(8,128)(2,1)}, f32[2,384,384]{2,1,0:T(8,128)S(1)}, bf16[2,384,384]{2,1,0:T(8,128)(2,1)S(1)}) custom-call(f32[1]{0:T(128)} %bitcast.2.bias_ref, bf16[384,1536]{1,0:T(8,128)(2,1)S(1)} %bitcast.89, bf16[384,1536]{1,0:T(8,128)(2,1)S(1)} %bitcast.69, bf16[384,1536]{1,0:T(8,128)(2,1)S(1)} %bitcast.81, ...), custom_call_target="tpu_custom_call" | custom-call | flops 1000 | bytes 1000 | tf_op jit(solution)/shard_map/attend_grad/pallas_call | solution.py:151
  77.8 1.0 constant_dynamic-slice_fusion.1
  79.9 1.8 %multiply_convert_fusion = bf16[768,768]{1,0:T(8,128)(2,1)} fusion(bf16[768,384]{1,0:T(8,128)(2,1)S(1)} %bitcast.109, bf16[384,1536]{1,0:T(8,128)(2,1)S(1)} %bitcast.98), kind=kOutput, calls=%fused_computation.2 | convolution fusion | flops 454164480 | bytes 2359296 | tf_op jit(solution)/shard_map/dot_general | solution.py:25
  81.7 1.8 %multiply_convert_fusion.1 = bf16[768,768]{1,0:T(8,128)(2,1)} fusion(bf16[768,384]{1,0:T(8,128)(2,1)S(1)} %bitcast.110, bf16[384,1536]{1,0:T(8,128)(2,1)S(1)} %bitcast.99), kind=kOutput, calls=%fused_computation.3 | convolution fusion | flops 454164480 | bytes 2359296 | tf_op jit(solution)/shard_map/dot_general | solution.py:25
  84.0 1.7 %collective-permute-start.6 = (bf16[2,384,384]{2,1,0:T(8,128)(2,1)}, bf16[2,384,384]{2,1,0:T(8,128)(2,1)S(1)}, u32[]{:S(2)}, u32[]{:S(2)}) collective-permute-start(bf16[2,384,384]{2,1,0:T(8,128)(2,1)} %copy-done.20), channel_id=1, source_target_pairs={{0,1},{1,0},{2,3},{3,2},{4,5},{5,4},{6,7},{7,6},{8,9},{9,8},{10,11... | collective-permute-start | bytes 1769480 | tf_op jit(solution)/shard_map/ppermute | solution.py:31
  86.5 10.3 %attend_grad.5 = (bf16[384,1536]{1,0:T(8,128)(2,1)}, f32[2,384,512]{2,1,0:T(8,128)}, bf16[2,384,512]{2,1,0:T(8,128)(2,1)}) custom-call(f32[1]{0:T(128)} %bitcast.2.bias_ref, bf16[384,1536]{1,0:T(8,128)(2,1)S(1)} %bitcast.90, bf16[384,1536]{1,0:T(8,128)(2,1)S(1)} %bitcast.70, bf16[384,1536]{1,0:T(8,128)(2,1)S(1)} %bitcast.82, ...), custom_call_target="tpu_custom_call", output_to_operand_aliasing={{0}: (9, {})} | custom-call | flops 1000 | bytes 1000 | tf_op jit(solution)/shard_map/attend_grad/pallas_call | solution.py:151
  98.7 1.1 collective-permute-done.6.refs_0_
  99.8 1.8 %copy_add_fusion = f32[2,2,2,96,768]{4,3,2,0,1:T(8,128)S(1)} fusion(f32[2,2,2,96,768]{4,3,2,1,0:T(8,128)S(1)} %bitcast.106, bf16[2,2,2,96,768]{4,3,2,1,0:T(8,128)(2,1)} %bitcast.20), kind=kLoop, calls=%fused_computation | loop fusion | flops 1179648 | bytes 5898240 | tf_op jit(solution)/shard_map/add | solution.py:238
  101.6 1.0 fusion.1
  102.6 1.7 %collective-permute-start.8 = (bf16[2,2,96,768]{3,2,1,0:T(8,128)(2,1)}, bf16[2,2,96,768]{3,2,1,0:T(8,128)(2,1)}, u32[]{:S(2)}, u32[]{:S(2)}) collective-permute-start(bf16[2,2,96,768]{3,2,1,0:T(8,128)(2,1)} %fusion.1), channel_id=1, source_target_pairs={{0,8},{2,10},{4,12},{6,14},{8,0},{10,2},{12,4},{14,6},{16,24},{18,... | collective-permute-start | bytes 1769480 | tf_op jit(solution)/shard_map/ppermute | solution.py:194
  104.3 1.6 copy_add_fusion.1
  106.0 1.0 fusion
  107.6 1.5 collective-permute-start.7
  109.8 8.4 %attend_grad.6 = (bf16[384,1536]{1,0:T(8,128)(2,1)}, f32[2,384,384]{2,1,0:T(8,128)S(1)}, bf16[2,384,384]{2,1,0:T(8,128)(2,1)}) custom-call(f32[1]{0:T(128)} %bitcast.2.bias_ref, bf16[384,1536]{1,0:T(8,128)(2,1)S(1)} %bitcast.91, bf16[384,1536]{1,0:T(8,128)(2,1)S(1)} %bitcast.71, bf16[384,1536]{1,0:T(8,128)(2,1)S(1)} %bitcast.83, ...), custom_call_target="tpu_custom_call", output_to_operand_aliasing={{0}: (9, {})} | custom-call | flops 1000 | bytes 1000 | tf_op jit(solution)/shard_map/attend_grad/pallas_call | solution.py:151
  118.2 2.3 %collective-permute-start.12 = (bf16[2,384,384]{2,1,0:T(8,128)(2,1)}, bf16[2,384,384]{2,1,0:T(8,128)(2,1)}, u32[]{:S(2)}, u32[]{:S(2)}) collective-permute-start(bf16[2,384,384]{2,1,0:T(8,128)(2,1)} %get-tuple-element.74), channel_id=1, source_target_pairs={{0,1},{1,0},{2,3},{3,2},{4,5},{5,4},{6,7},{7,6},{8,9},{9,8},{10,11... | collective-permute-start | bytes 1769480 | tf_op jit(solution)/shard_map/ppermute | solution.py:31
  120.6 1.3 collective-permute-done.7
  121.8 1.2 bitcast_add_fusion
  123.0 1.6 bitcast_add_fusion.1
  126.3 2.5 %collective-permute-start.11 = (bf16[2,96,768]{2,1,0:T(8,128)(2,1)}, bf16[2,96,768]{2,1,0:T(8,128)(2,1)}, u32[]{:S(2)}, u32[]{:S(2)}) collective-permute-start(bf16[2,96,768]{2,1,0:T(8,128)(2,1)} %fusion.7), channel_id=1, source_target_pairs={{0,16},{2,18},{4,20},{6,22},{8,24},{10,26},{12,28},{14,30},{16,0},... | collective-permute-start | bytes 884744 | tf_op jit(solution)/shard_map/ppermute | solution.py:194
  130.0 6.2 %attend_grad.7 = (bf16[384,1536]{1,0:T(8,128)(2,1)}, f32[2,384,256]{2,1,0:T(8,128)S(1)}, bf16[2,384,256]{2,1,0:T(8,128)(2,1)S(1)}) custom-call(f32[1]{0:T(128)} %bitcast.2.bias_ref, bf16[384,1536]{1,0:T(8,128)(2,1)S(1)} %bitcast.92, bf16[384,1536]{1,0:T(8,128)(2,1)S(1)} %bitcast.72, bf16[384,1536]{1,0:T(8,128)(2,1)S(1)} %bitcast.84, ...), custom_call_target="tpu_custom_call", output_to_operand_aliasing={{0}: (9, {})} | custom-call | flops 1000 | bytes 1000 | tf_op jit(solution)/shard_map/attend_grad/pallas_call | solution.py:151
  136.3 1.5 collective-permute-start.15
  137.8 2.6 %collective-permute-done.11 = bf16[2,96,768]{2,1,0:T(8,128)(2,1)} collective-permute-done((bf16[2,96,768]{2,1,0:T(8,128)(2,1)}, bf16[2,96,768]{2,1,0:T(8,128)(2,1)}, u32[]{:S(2)}, u32[]{:S(2)}) %collective-permute-start.11) | collective-permute-done | bytes 294944 | tf_op jit(solution)/shard_map/ppermute | solution.py:194
  140.4 1.4 collective-permute-done.10
  141.7 1.0 bitcast_add_fusion.3
  142.9 1.1 bitcast_add_fusion.2
  144.1 1.6 collective-permute-start.14
  145.6 1.5 add_parts.4
  147.2 3.4 %add_parts.5 = (bf16[384,1536]{1,0:T(8,128)(2,1)}, bf16[384,1536]{1,0:T(8,128)(2,1)}) custom-call(f32[2,384,512]{2,1,0:T(8,128)S(1)} %copy-done.5, bf16[2,384,512]{2,1,0:T(8,128)(2,1)} %collective-permute-done.9.refs_0_, bf16[384,1536]{1,0:T(8,128)(2,1)} %get-tuple-element.92.refs_1_, ...), custom_call_target="tpu_custom_call", output_to_operand_aliasing={{0}: (2, {}), {1}: (3, {})} | custom-call | bytes 3145728 | tf_op jit(solution)/shard_map/add_parts/pallas_call | solution.py:179
  151.5 1.3 collective-permute-start.17
  152.8 2.8 %add_parts.6 = (bf16[384,1536]{1,0:T(8,128)(2,1)}, bf16[384,1536]{1,0:T(8,128)(2,1)}) custom-call(f32[2,384,384]{2,1,0:T(8,128)S(1)} %copy-done.9, bf16[2,384,384]{2,1,0:T(8,128)(2,1)} %collective-permute-done.12.refs_0_, bf16[384,1536]{1,0:T(8,128)(2,1)} %get-tuple-element.94.refs_1_, ...), custom_call_target="tpu_custom_call", output_to_operand_aliasing={{0}: (2, {}), {1}: (3, {})} | custom-call | bytes 2359296 | tf_op jit(solution)/shard_map/add_parts/pallas_call | solution.py:179
  155.6 0.9 add_parts.7
  156.5 1.3 collective-permute-done.17
  157.9 0.9 pad_maximum_fusion.3
  (104 shorter events, 15.7 us)
Async XLA Ops:
  7.2 61.5 %all-gather.2.cloned.1.call-start = ((), (), s32[]{:S(2)}) async-start(), calls=%async_computation | async-start | bytes 5013504 | tf_op jit(solution)/shard_map/all_gather | solution.py:269
  7.9 5.1 %copy-start.1 = (bf16[1,384,1536]{2,1,0:T(8,128)(2,1)S(1)}, bf16[1,384,1536]{2,1,0:T(8,128)(2,1)}, u32[]{:S(2)}) copy-start(bf16[1,384,1536]{2,1,0:T(8,128)(2,1)} %param.9) | copy-start | bytes 3538948
  9.1 3.9 %copy-start = (bf16[1,384,1536]{2,1,0:T(8,128)(2,1)S(1)}, bf16[1,384,1536]{2,1,0:T(8,128)(2,1)}, u32[]{:S(2)}) copy-start(bf16[1,384,1536]{2,1,0:T(8,128)(2,1)} %param.8) | copy-start | bytes 3538948
  10.0 17.4 %collective-permute-start.3 = (bf16[2,384,384]{2,1,0:T(8,128)(2,1)}, bf16[2,384,384]{2,1,0:T(8,128)(2,1)}, u32[]{:S(2)}, u32[]{:S(2)}) collective-permute-start(bf16[2,384,384]{2,1,0:T(8,128)(2,1)} %pad_maximum_fusion.1), channel_id=1, source_target_pairs={{0,1},{1,0},{2,3},{3,2},{4,5},{5,4},{6,7},{7,6},{8,9},{9,8},{10,11... | collective-permute-start | bytes 1769480 | tf_op jit(solution)/shard_map/ppermute | solution.py:31
  14.0 30.3 %collective-permute-start.2 = (bf16[2,384,512]{2,1,0:T(8,128)(2,1)}, bf16[2,384,512]{2,1,0:T(8,128)(2,1)}, u32[]{:S(2)}, u32[]{:S(2)}) collective-permute-start(bf16[2,384,512]{2,1,0:T(8,128)(2,1)} %pad_maximum_fusion), channel_id=1, source_target_pairs={{0,1},{1,0},{2,3},{3,2},{4,5},{5,4},{6,7},{7,6},{8,9},{9,8},{10,11... | collective-permute-start | bytes 2359304 | tf_op jit(solution)/shard_map/ppermute | solution.py:31
  14.7 4.4 %copy-start.32 = (s32[2,3]{1,0:T(2,128)S(1)}, s32[2,3]{1,0:T(2,128)}, u32[]{:S(2)}) copy-start(s32[2,3]{1,0:T(2,128)} %param.13) | copy-start | bytes 76
  14.7 12.8 %copy-start.2 = (bf16[1,384,1536]{2,1,0:T(8,128)(2,1)S(1)}, bf16[1,384,1536]{2,1,0:T(8,128)(2,1)}, u32[]{:S(2)}) copy-start(bf16[1,384,1536]{2,1,0:T(8,128)(2,1)} %param.7) | copy-start | bytes 3538948
  15.6 41.4 %collective-permute-start.1 = (bf16[2,384,384]{2,1,0:T(8,128)(2,1)}, bf16[2,384,384]{2,1,0:T(8,128)(2,1)}, u32[]{:S(2)}, u32[]{:S(2)}) collective-permute-start(bf16[2,384,384]{2,1,0:T(8,128)(2,1)} %pad_maximum_fusion.2), channel_id=1, source_target_pairs={{0,1},{1,0},{2,3},{3,2},{4,5},{5,4},{6,7},{7,6},{8,9},{9,8},{10,11... | collective-permute-start | bytes 1769480 | tf_op jit(solution)/shard_map/ppermute | solution.py:31
  17.8 46.7 %collective-permute-start = (bf16[2,384,256]{2,1,0:T(8,128)(2,1)}, bf16[2,384,256]{2,1,0:T(8,128)(2,1)}, u32[]{:S(2)}, u32[]{:S(2)}) collective-permute-start(bf16[2,384,256]{2,1,0:T(8,128)(2,1)} %pad_maximum_fusion.4), channel_id=1, source_target_pairs={{0,1},{1,0},{2,3},{3,2},{4,5},{5,4},{6,7},{7,6},{8,9},{9,8},{10,11... | collective-permute-start | bytes 1179656 | tf_op jit(solution)/shard_map/ppermute | solution.py:31
  48.7 11.7 %copy-start.12 = (f32[4,8,384]{2,1,0:T(8,128)}, f32[4,8,384]{2,1,0:T(8,128)S(1)}, u32[]{:S(2)}) copy-start(f32[4,8,384]{2,1,0:T(8,128)S(1)} %get-tuple-element.66.lse_ref) | copy-start | bytes 147460
  67.1 1.0 copy-start.3
  68.7 0.8 copy-start.17
  69.5 8.3 %copy-start.4 = (bf16[1536,384]{1,0:T(8,128)(2,1)S(1)}, bf16[1536,384]{1,0:T(8,128)(2,1)}, u32[]{:S(2)}) copy-start(bf16[1536,384]{1,0:T(8,128)(2,1)} %copy-done.3) | copy-start | bytes 3538948
  77.8 1.2 copy-start.6
  77.8 1.4 copy-start.20
  77.8 2.1 %copy-start.21 = (bf16[1,384,1536]{2,1,0:T(8,128)(2,1)S(1)}, bf16[1,384,1536]{2,1,0:T(8,128)(2,1)}, u32[]{:S(2)}) copy-start(bf16[1,384,1536]{2,1,0:T(8,128)(2,1)} %param.10) | copy-start | bytes 3538948
  83.5 16.3 %collective-permute-start.4 = (bf16[768,768]{1,0:T(8,128)(2,1)}, bf16[768,768]{1,0:T(8,128)(2,1)}, u32[]{:S(2)}, u32[]{:S(2)}) collective-permute-start(bf16[768,768]{1,0:T(8,128)(2,1)} %multiply_convert_fusion.1), channel_id=1, source_target_pairs={{0,2},{2,0},{4,6},{6,4},{8,10},{10,8},{12,14},{14,12},{16,18},{18,... | collective-permute-start | bytes 3538952 | tf_op jit(solution)/shard_map/ppermute | solution.py:194
  83.5 16.3 %collective-permute-start.5 = (bf16[768,768]{1,0:T(8,128)(2,1)}, bf16[768,768]{1,0:T(8,128)(2,1)}, u32[]{:S(2)}, u32[]{:S(2)}) collective-permute-start(bf16[768,768]{1,0:T(8,128)(2,1)} %multiply_convert_fusion), channel_id=1, source_target_pairs={{0,2},{2,0},{4,6},{6,4},{8,10},{10,8},{12,14},{14,12},{16,18},{18,... | collective-permute-start | bytes 3538952 | tf_op jit(solution)/shard_map/ppermute | solution.py:194
  84.0 15.8 %collective-permute-start.6 = (bf16[2,384,384]{2,1,0:T(8,128)(2,1)}, bf16[2,384,384]{2,1,0:T(8,128)(2,1)S(1)}, u32[]{:S(2)}, u32[]{:S(2)}) collective-permute-start(bf16[2,384,384]{2,1,0:T(8,128)(2,1)} %copy-done.20), channel_id=1, source_target_pairs={{0,1},{1,0},{2,3},{3,2},{4,5},{5,4},{6,7},{7,6},{8,9},{9,8},{10,11... | collective-permute-start | bytes 1769480 | tf_op jit(solution)/shard_map/ppermute | solution.py:31
  85.7 0.8 copy-start.13
  86.5 10.6 %copy-start.22 = (bf16[1,384,1536]{2,1,0:T(8,128)(2,1)S(1)}, bf16[1,384,1536]{2,1,0:T(8,128)(2,1)}, u32[]{:S(2)}) copy-start(bf16[1,384,1536]{2,1,0:T(8,128)(2,1)} %param.10) | copy-start | bytes 3538948
  86.5 10.6 %copy-start.27 = (bf16[8,1,96,384]{3,2,1,0:T(8,128)(2,1)S(1)}, bf16[8,1,96,384]{3,2,1,0:T(8,128)(2,1)}, u32[]{:S(2)}) copy-start(bf16[8,1,96,384]{3,2,1,0:T(8,128)(2,1)} %get-tuple-element.111) | copy-start | bytes 1769476
  96.8 23.7 %collective-permute-start.9 = (bf16[2,384,512]{2,1,0:T(8,128)(2,1)}, bf16[2,384,512]{2,1,0:T(8,128)(2,1)}, u32[]{:S(2)}, u32[]{:S(2)}) collective-permute-start(bf16[2,384,512]{2,1,0:T(8,128)(2,1)} %get-tuple-element.68), channel_id=1, source_target_pairs={{0,1},{1,0},{2,3},{3,2},{4,5},{5,4},{6,7},{7,6},{8,9},{9,8},{10,11... | collective-permute-start | bytes 2359304 | tf_op jit(solution)/shard_map/ppermute | solution.py:31
  99.7 1.8 %copy-start.10 = (bf16[2,384,384]{2,1,0:T(8,128)(2,1)}, bf16[2,384,384]{2,1,0:T(8,128)(2,1)S(1)}, u32[]{:S(2)}) copy-start(bf16[2,384,384]{2,1,0:T(8,128)(2,1)S(1)} %collective-permute-done.6.refs_0_) | copy-start | bytes 1769476
  101.6 4.4 %copy-start.23 = (f32[2,2,2,96,768]{4,3,2,0,1:T(8,128)}, f32[2,2,2,96,768]{4,3,2,0,1:T(8,128)S(1)}, u32[]{:S(2)}) copy-start(f32[2,2,2,96,768]{4,3,2,0,1:T(8,128)S(1)} %copy_add_fusion) | copy-start | bytes 7077892
  102.6 17.9 %collective-permute-start.8 = (bf16[2,2,96,768]{3,2,1,0:T(8,128)(2,1)}, bf16[2,2,96,768]{3,2,1,0:T(8,128)(2,1)}, u32[]{:S(2)}, u32[]{:S(2)}) collective-permute-start(bf16[2,2,96,768]{3,2,1,0:T(8,128)(2,1)} %fusion.1), channel_id=1, source_target_pairs={{0,8},{2,10},{4,12},{6,14},{8,0},{10,2},{12,4},{14,6},{16,24},{18,... | collective-permute-start | bytes 1769480 | tf_op jit(solution)/shard_map/ppermute | solution.py:194
  105.9 1.6 copy-start.25
  107.6 14.2 %collective-permute-start.7 = (bf16[2,2,96,768]{3,2,0,1:T(8,128)(2,1)}, bf16[2,2,96,768]{3,2,0,1:T(8,128)(2,1)}, u32[]{:S(2)}, u32[]{:S(2)}) collective-permute-start(bf16[2,2,96,768]{3,2,0,1:T(8,128)(2,1)} %fusion), channel_id=1, source_target_pairs={{0,4},{2,6},{4,0},{6,2},{8,12},{10,14},{12,8},{14,10},{16,20},{18,... | collective-permute-start | bytes 1769480 | tf_op jit(solution)/shard_map/ppermute | solution.py:194
  109.1 0.8 copy-start.15
  109.8 12.0 %copy-start.24 = (f32[2,2,2,96,768]{4,3,2,0,1:T(8,128)S(1)}, f32[2,2,2,96,768]{4,3,2,0,1:T(8,128)}, u32[]{:S(2)}) copy-start(f32[2,2,2,96,768]{4,3,2,0,1:T(8,128)} %copy-done.23) | copy-start | bytes 7077892
  118.2 4.8 %copy-start.8 = (f32[2,384,384]{2,1,0:T(8,128)}, f32[2,384,384]{2,1,0:T(8,128)S(1)}, u32[]{:S(2)}) copy-start(f32[2,384,384]{2,1,0:T(8,128)S(1)} %get-tuple-element.87.own_ref) | copy-start | bytes 3538948
  118.2 4.8 %copy-start.26 = (f32[2,2,2,96,768]{4,3,0,1,2:T(8,128)S(1)}, f32[2,2,2,96,768]{4,3,0,1,2:T(8,128)}, u32[]{:S(2)}) copy-start(f32[2,2,2,96,768]{4,3,0,1,2:T(8,128)} %copy-done.25) | copy-start | bytes 7077892
  118.2 19.6 %collective-permute-start.12 = (bf16[2,384,384]{2,1,0:T(8,128)(2,1)}, bf16[2,384,384]{2,1,0:T(8,128)(2,1)}, u32[]{:S(2)}, u32[]{:S(2)}) collective-permute-start(bf16[2,384,384]{2,1,0:T(8,128)(2,1)} %get-tuple-element.74), channel_id=1, source_target_pairs={{0,1},{1,0},{2,3},{3,2},{4,5},{5,4},{6,7},{7,6},{8,9},{9,8},{10,11... | collective-permute-start | bytes 1769480 | tf_op jit(solution)/shard_map/ppermute | solution.py:31
  123.0 2.5 %copy-start.28 = (f32[2,2,96,768]{3,2,1,0:T(8,128)}, f32[2,2,96,768]{3,2,1,0:T(8,128)S(1)}, u32[]{:S(2)}) copy-start(f32[2,2,96,768]{3,2,1,0:T(8,128)S(1)} %bitcast_add_fusion) | copy-start | bytes 3538948
  124.7 1.6 copy-start.30
  126.3 14.1 %collective-permute-start.11 = (bf16[2,96,768]{2,1,0:T(8,128)(2,1)}, bf16[2,96,768]{2,1,0:T(8,128)(2,1)}, u32[]{:S(2)}, u32[]{:S(2)}) collective-permute-start(bf16[2,96,768]{2,1,0:T(8,128)(2,1)} %fusion.7), channel_id=1, source_target_pairs={{0,16},{2,18},{4,20},{6,22},{8,24},{10,26},{12,28},{14,30},{16,0},... | collective-permute-start | bytes 884744 | tf_op jit(solution)/shard_map/ppermute | solution.py:194
  128.8 12.9 %collective-permute-start.10 = (bf16[2,96,768]{2,1,0:T(8,128)(2,1)}, bf16[2,96,768]{2,1,0:T(8,128)(2,1)}, u32[]{:S(2)}, u32[]{:S(2)}) collective-permute-start(bf16[2,96,768]{2,1,0:T(8,128)(2,1)} %fusion.6), channel_id=1, source_target_pairs={{0,8},{2,10},{4,12},{6,14},{8,0},{10,2},{12,4},{14,6},{16,24},{18,... | collective-permute-start | bytes 884744 | tf_op jit(solution)/shard_map/ppermute | solution.py:194
  130.0 11.7 %copy-start.31 = (f32[2,2,96,768]{3,2,0,1:T(8,128)S(1)}, f32[2,2,96,768]{3,2,0,1:T(8,128)}, u32[]{:S(2)}) copy-start(f32[2,2,96,768]{3,2,0,1:T(8,128)} %copy-done.30) | copy-start | bytes 3538948
  136.2 6.6 %copy-start.29 = (f32[2,2,96,768]{3,2,1,0:T(8,128)S(1)}, f32[2,2,96,768]{3,2,1,0:T(8,128)}, u32[]{:S(2)}) copy-start(f32[2,2,96,768]{3,2,1,0:T(8,128)} %copy-done.28) | copy-start | bytes 3538948
  136.3 19.3 %collective-permute-start.15 = (bf16[2,384,256]{2,1,0:T(8,128)(2,1)S(1)}, bf16[2,384,256]{2,1,0:T(8,128)(2,1)S(1)}, u32[]{:S(2)}, u32[]{:S(2)}) collective-permute-start(bf16[2,384,256]{2,1,0:T(8,128)(2,1)S(1)} %get-tuple-element.82), channel_id=1, source_target_pairs={{0,1},{1,0},{2,3},{3,2},{4,5},{5,4},{6,7},{7,6},{8,9},{9,8},{10,11... | collective-permute-start | bytes 1179656 | tf_op jit(solution)/shard_map/ppermute | solution.py:31
  142.8 2.9 %copy-start.7 = (f32[2,384,384]{2,1,0:T(8,128)S(1)}, f32[2,384,384]{2,1,0:T(8,128)}, u32[]{:S(2)}) copy-start(f32[2,384,384]{2,1,0:T(8,128)} %copy-done.6) | copy-start | bytes 3538948
  142.8 2.9 %copy-start.11 = (bf16[2,384,384]{2,1,0:T(8,128)(2,1)S(1)}, bf16[2,384,384]{2,1,0:T(8,128)(2,1)}, u32[]{:S(2)}) copy-start(bf16[2,384,384]{2,1,0:T(8,128)(2,1)} %copy-done.10) | copy-start | bytes 1769476
  142.8 7.8 %collective-permute-start.13 = (bf16[96,768]{1,0:T(8,128)(2,1)S(1)}, bf16[96,768]{1,0:T(8,128)(2,1)S(1)}, u32[]{:S(2)}, u32[]{:S(2)}) collective-permute-start(bf16[96,768]{1,0:T(8,128)(2,1)S(1)} %fusion.8), channel_id=1, source_target_pairs={{0,16},{2,18},{4,20},{6,22},{8,24},{10,26},{12,28},{14,30},{16,0},... | collective-permute-start | bytes 442376 | tf_op jit(solution)/shard_map/ppermute | solution.py:194
  144.0 3.2 %copy-start.5 = (f32[2,384,512]{2,1,0:T(8,128)S(1)}, f32[2,384,512]{2,1,0:T(8,128)}, u32[]{:S(2)}) copy-start(f32[2,384,512]{2,1,0:T(8,128)} %get-tuple-element.89.own_ref) | copy-start | bytes 4718596
  144.1 7.4 %collective-permute-start.14 = (bf16[96,768]{1,0:T(8,128)(2,1)S(1)}, bf16[96,768]{1,0:T(8,128)(2,1)S(1)}, u32[]{:S(2)}, u32[]{:S(2)}) collective-permute-start(bf16[96,768]{1,0:T(8,128)(2,1)S(1)} %fusion.9), channel_id=1, source_target_pairs={{0,4},{2,6},{4,0},{6,2},{8,12},{10,14},{12,8},{14,10},{16,20},{18,... | collective-permute-start | bytes 442376 | tf_op jit(solution)/shard_map/ppermute | solution.py:194
  150.6 2.2 %copy-start.9 = (f32[2,384,384]{2,1,0:T(8,128)S(1)}, f32[2,384,384]{2,1,0:T(8,128)}, u32[]{:S(2)}) copy-start(f32[2,384,384]{2,1,0:T(8,128)} %copy-done.8) | copy-start | bytes 3538948
  150.6 5.9 %collective-permute-start.16 = (bf16[96,768]{1,0:T(8,128)(2,1)S(1)}, bf16[96,768]{1,0:T(8,128)(2,1)S(1)}, u32[]{:S(2)}, u32[]{:S(2)}) collective-permute-start(bf16[96,768]{1,0:T(8,128)(2,1)S(1)} %bitcast_add_fusion.5), channel_id=1, source_target_pairs={{0,1},{1,0},{2,3},{3,2},{4,5},{5,4},{6,7},{7,6},{8,9},{9,8},{10,11... | collective-permute-start | bytes 442376 | tf_op jit(solution)/shard_map/ppermute | solution.py:31
  151.5 6.3 %collective-permute-start.17 = (bf16[96,768]{1,0:T(8,128)(2,1)S(1)}, bf16[96,768]{1,0:T(8,128)(2,1)S(1)}, u32[]{:S(2)}, u32[]{:S(2)}) collective-permute-start(bf16[96,768]{1,0:T(8,128)(2,1)S(1)} %bitcast_add_fusion.4), channel_id=1, source_target_pairs={{0,1},{1,0},{2,3},{3,2},{4,5},{5,4},{6,7},{7,6},{8,9},{9,8},{10,11... | collective-permute-start | bytes 442376 | tf_op jit(solution)/shard_map/ppermute | solution.py:31
  (4 other events, 2.6 us)
Sparse Core Ops, SparseCore 0:
  10.3 55.9 all-gather.1
